TPU v7x, 32 devices: a whole 2x2x4 slice. The times are simulated.
32 devices in a mesh: wide: 8 (over y, x, core), narrow: 4 (over z).
Axes of the slice: x: 2, y: 2, z: 4, core: 2. Of those that a mesh axis runs over, the one named last changes fastest.
Arguments:
- coarse_basis: bfloat16 [16, 96, 3, 16, 8, 128], P('wide', None, None, 'narrow')
- material_ids: int32 [16, 16, 8, 128], P('wide', 'narrow'), may hold values from 0 to 15
- lame_table: bfloat16 [2, 16], replicated, may hold values from 0.5 to 4
- coarse_ids: int32 [16, 96], P('wide'), may hold values from 0 to 127, as said below
- coarse_slab: bfloat16 [98304, 512], P('wide', 'narrow'), may hold values from -0.5 to 2.5, as said below
- panel_owner: int32 [1], replicated, may hold values from 0 to 2
Outputs:
- factored: bfloat16 [98304, 512], P('wide', 'narrow')
- galerkin: float32 [16, 96, 96], P('wide')
Inputs may be any that keep to these rules, and one draw needn't show every extreme that they name: `coarse_ids`: the 96 numbers of a row are distinct. `coarse_slab`: for every column block t, the 128 x 128 block whose rows begin at t * 2 * 12288 is symmetric positive definite.
All inputs are finite; a program needn't handle non-finite values.
Results may differ from a plain program's by a relative error of at most 0.001.
The roundings to bfloat16 on the way count: a program that leaves them out, or rounds other values in their place, can miss the bound.
Values may be sent and summed in bfloat16 or wider, within the bound.
No kernel may reach another device: no remote copies, remote signals or barrier semaphores. Data moves between devices by JAX's collectives and lax.ppermute only.
A program may use at most 192 MiB of HBM per device.

v0:
```python
import functools

import jax
import jax.numpy as jnp
from jax import lax
from jax.experimental import pallas as pl
from jax.experimental.pallas import tpu as pltpu
from jax.sharding import PartitionSpec as P

F32, BF16 = jnp.float32, jnp.bfloat16
NT = (((1,), (1,)), ((), ()))
TN = (((0,), (0,)), ((), ()))
VMEM = pl.BlockSpec(memory_space=pltpu.VMEM)
ANY = pl.BlockSpec(memory_space=pl.ANY)
SMEM = pl.BlockSpec(memory_space=pltpu.SMEM)
PLANS = {
    1: (
        (12, 6, 6),
        (),
        (
            "assemble", "next", "spread", "others", "spread", "more", "spread", (0, 0), "factor", "summary",
            "sums", ("panel", 0, 2), ("panel", 2, 3),
        ),
    ),
    2: (
        (12, 6, 4, 2),
        (),
        (
            "assemble", "next", "spread", "others", "spread", "more", "spread", (0, 0), (1, 0), "factor", (2, 0),
            "summary", ("panel", 1, 2), (3, 0), "sums", ("panel", 0, 1), ("panel", 2, 4),
        ),
    ),
    3: (
        (12, 6, 4, 2),
        (1, 2),
        (
            "assemble", "next", "spread", "others", "spread", "more", "spread", (0, 0), "factor", (1, 0), "summary",
            (0, 1), (1, 1), (2, 0), (2, 1), ("panel", 1, 2), (3, 0), (3, 1), "sums", ("panel", 0, 1), ("panel", 2, 4),
        ),
    ),
}
BLOCK = 16
LIGHT = pl.CostEstimate(flops=1, bytes_accessed=1, transcendentals=0)


def exact_dot(left, right, dims=(((1,), (0,)), ((), ()))):
    return lax.dot_general(
        left, right, dims, precision=lax.Precision.HIGHEST, preferred_element_type=F32
    )


def dot(left, right, dims=(((1,), (0,)), ((), ()))):
    return lax.dot_general(left, right, dims, preferred_element_type=F32)


def split_two(value):
    high = value.astype(BF16)
    return high, (value - high.astype(F32)).astype(BF16)


def lame_of(ids, table_ref):
    shear = jnp.zeros(ids.shape, F32)
    dilate = jnp.zeros(ids.shape, F32)
    for material in range(table_ref.shape[1]):
        chosen = ids == material
        shear = jnp.where(chosen, table_ref[0, material], shear)
        dilate = jnp.where(chosen, table_ref[1, material], dilate)
    return shear, dilate


def halo_kernel(table_ref, ids_ref, token_ref, basis_ref, slab_ref, out_ref, last_ref, *rest, spans):
    piece_refs, sems = rest[:-1], rest[-1]
    subs, funcs, comps, layers = basis_ref.shape[0:4]
    copies = []
    for number, ((low, high), piece_ref) in enumerate(zip(spans, piece_refs)):
        copies.append(pltpu.make_async_copy(slab_ref.at[pl.ds(low, high - low)], piece_ref, sems.at[number]))
        copies[-1].start()
    for sub in range(subs):
        for comp in range(comps):
            out_ref[sub, comp * funcs : (comp + 1) * funcs] = basis_ref[sub, :, comp, 0]
            last_ref[sub, comp * funcs : (comp + 1) * funcs] = basis_ref[sub, :, comp, layers - 1]
        shear, dilate = lame_of(ids_ref[sub, 0], table_ref)
        out_ref[sub, comps * funcs] = shear.astype(BF16)
        out_ref[sub, comps * funcs + 1] = dilate.astype(BF16)
    for copy in copies:
        copy.wait()


def halo_message(table, ids, token, basis, slab, spans):
    subs, funcs, comps, layers, ny, nz = basis.shape
    return pl.pallas_call(
        functools.partial(halo_kernel, spans=spans),
        in_specs=[SMEM, VMEM, ANY, VMEM, ANY],
        out_specs=[VMEM] * (2 + len(spans)),
        out_shape=[
            jax.ShapeDtypeStruct((subs, comps * funcs + 2, ny, nz), BF16),
            jax.ShapeDtypeStruct((subs, comps * funcs, ny, nz), BF16),
        ]
        + [jax.ShapeDtypeStruct((high - low, slab.shape[1]), BF16) for low, high in spans],
        scratch_shapes=[pltpu.SemaphoreType.DMA((max(1, len(spans)),))],
        compiler_params=pltpu.CompilerParams(vmem_limit_bytes=16 * 2**20),
        cost_estimate=LIGHT,
        name="halo_message",
    )(table, ids, token, basis, slab)


def interior_kernel(edge_ref, table_ref, ids_ref, basis_ref, token_ref, out_ref, fields, turned, coef, left, right, acc):
    sub, comp = pl.program_id(0), pl.program_id(1)
    layers, ny, nz = basis_ref.shape[3:]
    funcs = basis_ref.shape[1]
    row = lax.broadcasted_iota(jnp.int32, (ny, nz), 0)
    lane = lax.broadcasted_iota(jnp.int32, (ny, nz), 1)
    table = [lame_of(ids_ref[sub, x], table_ref) for x in range(layers)]

    def weight(one, two, direction):
        shear = 0.5 * (one[0] + two[0])
        dilate = 0.5 * (one[1] + two[1])
        return shear + jnp.where(comp == direction, shear + dilate, 0.0)

    def ahead(field, axis):
        size = field.shape[axis]
        index = row if axis == 0 else lane
        return jnp.where(index == size - 1, 0.0, pltpu.roll(field, size - 1, axis=axis))

    def behind(field, axis):
        index = row if axis == 0 else lane
        return jnp.where(index == 0, 0.0, pltpu.roll(field, 1, axis=axis))

    nothing = (jnp.zeros((ny, nz), F32),) * 2
    previous = weight(table[0], nothing, 0) * edge_ref[0].astype(F32)
    for x in range(layers):
        diagonal = previous
        forward = []
        if x + 1 < layers:
            face = weight(table[x], table[x + 1], 0)
            diagonal = diagonal + face
            previous = face
            forward.append(face)
        else:
            forward.append(jnp.zeros((ny, nz), F32))
        for axis in (0, 1):
            index, size = (row, ny) if axis == 0 else (lane, nz)
            other = tuple(ahead(value, axis) for value in table[x])
            face = weight(table[x], other, axis + 1)
            before = tuple(behind(value, axis) for value in table[x])
            diagonal = diagonal + face + weight(table[x], before, axis + 1)
            forward.append(jnp.where(index == size - 1, 0.0, face))
        coef[x, 0] = 0.5 * diagonal
        for kind in range(3):
            coef[x, kind + 1] = forward[kind]
        fields[x] = basis_ref[sub, :, comp, x].astype(F32).reshape(funcs * ny, nz)

    total = None
    for x in reversed(range(layers)):
        values = [fields[x, pl.ds(y, funcs, stride=ny), :] for y in range(ny)]
        for y in range(ny):
            value = values[y]
            turned[x % 2, y] = value
            image = coef[x, 0, y : y + 1, :] * value
            image = image - coef[x, 3, y : y + 1, :] * pltpu.roll(value, nz - 1, axis=1)
            if y + 1 < ny:
                image = image - coef[x, 2, y : y + 1, :] * values[y + 1]
            if x + 1 < layers:
                image = image - coef[x, 1, y : y + 1, :] * turned[(x + 1) % 2, y]
            high, low = split_two(image)
            left[:, y * nz : (y + 1) * nz] = value.astype(BF16)
            right[0:funcs, y * nz : (y + 1) * nz] = high
            right[funcs : 2 * funcs, y * nz : (y + 1) * nz] = low
        product = dot(right[...], left[...], NT)
        total = product if total is None else total + product

    @pl.when(comp == 0)
    def _():
        acc[...] = total

    @pl.when(comp > 0)
    def _():
        acc[...] += total

    @pl.when(comp == pl.num_programs(1) - 1)
    def _():
        out_ref[0] = acc[0:funcs] + acc[funcs : 2 * funcs]


def interior(edge, table, ids, basis, token):
    subs, funcs, comps, layers, ny, nz = basis.shape
    return pl.pallas_call(
        interior_kernel,
        grid=(subs, comps),
        in_specs=[SMEM, SMEM, VMEM, VMEM, ANY],
        out_specs=pl.BlockSpec((1, funcs, funcs), lambda s, c: (s, 0, 0)),
        out_shape=jax.ShapeDtypeStruct((subs, funcs, funcs), F32),
        scratch_shapes=[
            pltpu.VMEM((layers, funcs * ny, nz), F32),
            pltpu.VMEM((2, ny, funcs, nz), F32),
            pltpu.VMEM((layers, 4, ny, nz), F32),
            pltpu.VMEM((funcs, ny * nz), BF16),
            pltpu.VMEM((2 * funcs, ny * nz), BF16),
            pltpu.VMEM((2 * funcs, funcs), F32),
        ],
        compiler_params=pltpu.CompilerParams(vmem_limit_bytes=16 * 2**20),
        cost_estimate=LIGHT,
        name="interior",
    )(edge, table, ids, basis, token)


def face_kernel(flags_ref, table_ref, ids_ref, last_ref, halo_ref, token_ref, inner_ref, out_ref, *scratch):
    @pl.when(flags_ref[0] == 1)
    def _():
        last, halo, sems = scratch[-3:]
        copies = [
            pltpu.make_async_copy(last_ref, last, sems.at[0]),
            pltpu.make_async_copy(halo_ref, halo, sems.at[1]),
        ]
        for copy in copies:
            copy.start()
        for copy in copies:
            copy.wait()
        face_sums(table_ref, ids_ref, last, halo, inner_ref, out_ref, *scratch[:-3])


def face_sums(table_ref, ids_ref, last_ref, halo_ref, inner_ref, out_ref, mine, theirs, left, right, weights, acc):
    subs, layers, ny, nz = ids_ref.shape
    funcs = inner_ref.shape[1]
    comps = last_ref.shape[1] // funcs

    @pl.loop(0, subs)
    def _(sub):
        shear, dilate = lame_of(ids_ref[sub, layers - 1], table_ref)
        weights[0] = 0.5 * (shear + halo_ref[sub, comps * funcs].astype(F32))
        weights[1] = 0.5 * (dilate + halo_ref[sub, comps * funcs + 1].astype(F32))

        @pl.loop(0, comps)
        def _(comp):
            weight = weights[0] + jnp.where(comp == 0, weights[0] + weights[1], 0.0)
            rows = pl.ds(comp * funcs, funcs)
            mine[...] = last_ref[sub, rows].astype(F32).reshape(funcs * ny, nz)
            theirs[...] = halo_ref[sub, rows].astype(F32).reshape(funcs * ny, nz)
            for y in range(ny):
                here = mine[pl.ds(y, funcs, stride=ny), :]
                there = theirs[pl.ds(y, funcs, stride=ny), :]
                high, low = split_two(weight[y : y + 1, :] * (here - there))
                left[0:funcs, y * nz : (y + 1) * nz] = here.astype(BF16)
                left[funcs : 2 * funcs, y * nz : (y + 1) * nz] = there.astype(BF16)
                right[0:funcs, y * nz : (y + 1) * nz] = high
                right[funcs : 2 * funcs, y * nz : (y + 1) * nz] = low
            product = dot(right[...], left[...], NT)

            @pl.when(comp == 0)
            def _():
                acc[...] = product

            @pl.when(comp > 0)
            def _():
                acc[...] += product

        total = acc[:, 0:funcs] - acc[:, funcs : 2 * funcs]
        half = inner_ref[sub] + 0.5 * (total[0:funcs] + total[funcs : 2 * funcs])
        out_ref[sub] = half + half.T


def face(flags, table, ids, last, halo, token, inner):
    subs, layers, ny, nz = ids.shape
    funcs = inner.shape[1]
    return pl.pallas_call(
        face_kernel,
        in_specs=[SMEM, SMEM, VMEM, ANY, ANY, ANY, VMEM],
        out_specs=VMEM,
        out_shape=jax.ShapeDtypeStruct((subs, funcs, funcs), F32),
        scratch_shapes=[
            pltpu.VMEM((funcs * ny, nz), F32),
            pltpu.VMEM((funcs * ny, nz), F32),
            pltpu.VMEM((2 * funcs, ny * nz), BF16),
            pltpu.VMEM((2 * funcs, ny * nz), BF16),
            pltpu.VMEM((2, ny, nz), F32),
            pltpu.VMEM((2 * funcs, 2 * funcs), F32),
            pltpu.VMEM(last.shape, BF16),
            pltpu.VMEM(halo.shape, BF16),
            pltpu.SemaphoreType.DMA((2,)),
        ],
        compiler_params=pltpu.CompilerParams(vmem_limit_bytes=16 * 2**20),
        cost_estimate=LIGHT,
        name="face",
    )(flags, table, ids, last, halo, token, inner)


def spread(gal_ref, column_ids_ref, row_ids_ref, size):
    subs, funcs = column_ids_ref.shape[0:2]
    added = jnp.zeros((size, size), F32)
    lane = lax.broadcasted_iota(jnp.int32, (funcs, size), 1)
    row = lax.broadcasted_iota(jnp.int32, (size, funcs), 0)
    for sub in range(subs):
        slots = (column_ids_ref[sub] == lane).astype(F32)
        slots_t = (row_ids_ref[sub] == row).astype(F32)
        added = added + exact_dot(slots_t, exact_dot(gal_ref[sub], slots))
    return added


def assemble_kernel(flags_ref, token_ref, column_ids_ref, row_ids_ref, slab_ref, head_ref, *rest):
    gal_refs, (message_ref, sum_ref) = rest[:-2], rest[-2:]
    size = message_ref.shape[0]
    mode, own = flags_ref[0], flags_ref[1]
    message_ref[...] = jnp.zeros_like(message_ref)

    @pl.when((mode == 1) & (own == 1))
    def _():
        total = gal_refs[0][...]
        for gal_ref in gal_refs[1:]:
            total = total + gal_ref[...]
        sum_ref[...] = total
        added = spread(sum_ref, column_ids_ref, row_ids_ref, size)
        message_ref[...] = added + slab_ref[...].astype(F32)

    @pl.when((mode == 2) & (own == 1))
    def _():
        message_ref[...] = head_ref[...].astype(F32)


def assemble(flags, token, ids, slab, head, parts):
    size = slab.shape[1]
    block = pl.BlockSpec((size, size), lambda i: (0, 0))
    return pl.pallas_call(
        assemble_kernel,
        grid=(1,),
        in_specs=[SMEM, ANY, VMEM, VMEM, block, block] + [VMEM] * len(parts),
        out_specs=VMEM,
        out_shape=jax.ShapeDtypeStruct((size, size), F32),
        scratch_shapes=[pltpu.VMEM(parts[0].shape, F32)],
        cost_estimate=LIGHT,
        name="assemble",
    )(flags, token, ids[:, :, None], ids[:, None, :], slab, head, *parts)


def factor_kernel(flags_ref, token_ref, *refs, parts, groups):
    message_refs, gal_refs = refs[:parts], refs[parts:-4]
    summary_ref, block_ref, sum_ref, work = refs[-4:]
    subs, funcs = gal_refs[0].shape[0:2]
    size = summary_ref.shape[1]
    diagonal = message_refs[0][...]
    for message_ref in message_refs[1:]:
        diagonal = diagonal + message_ref[...]
    block_ref[...] = diagonal

    @pl.when(flags_ref[0] == 1)
    def _():
        row = lax.broadcasted_iota(jnp.int32, (size, size), 0)
        lane = lax.broadcasted_iota(jnp.int32, (size, size), 1)
        work[:, 0:size] = 0.5 * (diagonal + diagonal.T)
        work[:, size : 2 * size] = (row == lane).astype(F32)
        index = lax.broadcasted_iota(jnp.int32, (BLOCK, size), 0)
        for start in range(0, size, BLOCK):
            panel = work[start : start + BLOCK, 0:size]
            extra = work[start : start + BLOCK, size : 2 * size]
            columns = [
                jnp.broadcast_to(panel[:, start + step : start + step + 1], (BLOCK, size))
                for step in range(BLOCK)
            ]
            for step in range(BLOCK):
                scale = lax.rsqrt(columns[step][step : step + 1, :])
                column = jnp.where(index > step, columns[step] * scale, 0.0)
                for later in range(step + 1, BLOCK):
                    columns[later] = columns[later] - column * column[later : later + 1, :]
                pivot = panel[step : step + 1, :] * scale
                panel = jnp.where(index == step, pivot, panel - column * pivot)
                pivot = extra[step : step + 1, :] * scale
                extra = jnp.where(index == step, pivot, extra - column * pivot)
            work[start : start + BLOCK, 0:size] = panel
            work[start : start + BLOCK, size : 2 * size] = extra
            rest = start + BLOCK
            if rest < size:
                both = jnp.concatenate([panel, extra], axis=1)
                work[rest:size, :] -= exact_dot(panel[:, rest:size], both, TN)
        upper = jnp.where(row <= lane, work[:, 0:size], 0.0)
        inverse = jnp.where(row >= lane, work[:, size : 2 * size], 0.0).T
        high = inverse.astype(BF16)
        summary_ref[0:size] = high
        summary_ref[size : 2 * size] = (inverse - high.astype(F32)).astype(BF16)
        summary_ref[2 * size : 3 * size] = upper.T.astype(BF16)
        each = len(gal_refs) // groups
        for group in range(groups):

            @pl.when(flags_ref[1] == group)
            def _(chosen=gal_refs[group * each : (group + 1) * each]):
                total = chosen[0][...]
                for gal_ref in chosen[1:]:
                    total = total + gal_ref[...]
                sum_ref[...] = total


def factorize(flags, token, messages, groups):
    size = messages[0].shape[1]
    subs, funcs = groups[0][0].shape[0:2]
    parts = [part for group in groups for part in group]
    return pl.pallas_call(
        functools.partial(factor_kernel, parts=len(messages), groups=len(groups)),
        in_specs=[SMEM, ANY] + [VMEM] * (len(messages) + len(parts)),
        out_specs=[VMEM] * 3,
        out_shape=[
            jax.ShapeDtypeStruct((3 * size, size), BF16),
            jax.ShapeDtypeStruct((size, size), F32),
            jax.ShapeDtypeStruct(groups[0][0].shape, F32),
        ],
        scratch_shapes=[pltpu.VMEM((size, 2 * size), F32)],
        cost_estimate=LIGHT,
        name="factorize",
    )(flags, token, *messages, *parts)


def prepare_kernel(flags_ref, token_ref, head_ref, *rest, sources):
    summary_refs = rest[:sources]
    weights_ref, rows_ref, lower_ref, summary, sem = rest[sources:]
    size = head_ref.shape[0]
    choice, mode = flags_ref[0], flags_ref[1]
    for number, summary_ref in enumerate(summary_refs):

        @pl.when(choice == number)
        def _(summary_ref=summary_ref):
            copy = pltpu.make_async_copy(summary_ref, summary, sem)
            copy.start()
            copy.wait()

    def doubled(block):
        nothing = jnp.zeros((size, size), BF16)
        top = jnp.concatenate([block, nothing], axis=1)
        return jnp.concatenate([top, jnp.concatenate([nothing, block], axis=1)], axis=0)

    @pl.when(mode > 0)
    def _():
        weights_ref[0 : 2 * size] = doubled(summary[0:size])
        weights_ref[2 * size : 4 * size] = doubled(summary[size : 2 * size])
        lower_ref[...] = summary[2 * size : 3 * size]

    @pl.when(mode == 2)
    def _():
        inverse = summary[0:size].astype(F32) + summary[size : 2 * size].astype(F32)
        solved = exact_dot(head_ref[...], inverse)
        rows_ref[...] = doubled(solved.T.astype(BF16))


def prepare(flags, token, head, summaries):
    size = head.shape[0]
    return pl.pallas_call(
        functools.partial(prepare_kernel, sources=len(summaries)),
        in_specs=[SMEM, ANY, VMEM] + [ANY] * len(summaries),
        out_specs=[VMEM] * 3,
        out_shape=[
            jax.ShapeDtypeStruct((4 * size, 2 * size), BF16),
            jax.ShapeDtypeStruct((2 * size, 2 * size), BF16),
            jax.ShapeDtypeStruct((size, size), BF16),
        ],
        scratch_shapes=[pltpu.VMEM(summaries[0].shape, BF16), pltpu.SemaphoreType.DMA],
        compiler_params=pltpu.CompilerParams(vmem_limit_bytes=16 * 2**20),
        cost_estimate=LIGHT,
        name="prepare",
    )(flags, token, head, *summaries)


def added_kernel(flags_ref, token_ref, column_ids_ref, row_ids_ref, *rest, sources):
    sum_refs, (added_ref, gal_ref) = rest[:sources], rest[sources:]
    for number, sum_ref in enumerate(sum_refs):

        @pl.when(flags_ref[0] == number)
        def _(sum_ref=sum_ref):
            gal_ref[...] = sum_ref[...]

    @pl.when((flags_ref[1] == 2) & (flags_ref[2] == 1))
    def _():
        added_ref[...] = spread(gal_ref, column_ids_ref, row_ids_ref, added_ref.shape[0])


def added_of(flags, token, ids, sums, size):
    return pl.pallas_call(
        functools.partial(added_kernel, sources=len(sums)),
        in_specs=[SMEM, ANY] + [VMEM] * (2 + len(sums)),
        out_specs=[VMEM] * 2,
        out_shape=[jax.ShapeDtypeStruct((size, size), F32), jax.ShapeDtypeStruct(sums[0].shape, F32)],
        cost_estimate=LIGHT,
        name="added",
    )(flags, token, ids[:, :, None], ids[:, None, :], *sums)


def panel_kernel(
    flags_ref, token_ref, lower_ref, weights_ref, rows_ref, added_ref, slab_ref, *rest, pieces, spans, first
):
    hops = len(pieces) // len(spans)
    others = rest[: len(pieces)]
    out_ref, done_ref, column, factor, sems = rest[-5:]
    done_ref[0] = flags_ref[0]
    tile, size = out_ref.shape
    half = tile // 2
    mode, head, own, which = flags_ref[0], flags_ref[1], flags_ref[2], flags_ref[3]
    step, steps = pl.program_id(0), pl.num_programs(0)
    top = first & (step == 0)

    def copy_of(at, act):
        for number, (begin, end) in enumerate(spans):
            for hop in range(hops):

                @pl.when((mode == 2) & (which == hop) & (at >= begin) & (at < end))
                def _(other_ref=others[number * hops + hop], begin=begin):
                    source = other_ref.at[pl.ds(pl.multiple_of((at - begin) * tile, tile), tile)]
                    act(pltpu.make_async_copy(source, column.at[at % 2], sems.at[at % 2]))

    @pl.when(step == 0)
    def _():
        copy_of(step, lambda copy: copy.start())

    @pl.when(step + 1 < steps)
    def _():
        copy_of(step + 1, lambda copy: copy.start())

    @pl.when(mode == 0)
    def _():
        out_ref[...] = slab_ref[...]

    @pl.when(mode == 1)
    def _():
        column[step % 2] = slab_ref[...]

    @pl.when(mode == 2)
    def _():
        copy_of(step, lambda copy: copy.wait())

    @pl.when(mode > 0)
    def _():
        value = column[step % 2]
        pair = jnp.concatenate([value[0:half], value[half:tile]], axis=1)
        factor[...] = dot(jnp.concatenate([pair, pair], axis=1), weights_ref[...]).astype(BF16)

        @pl.when(top & (head == 1))
        def _():
            factor[0:size, 0:size] = lower_ref[...]

        @pl.when(top & (head == 2))
        def _():
            factor[0:size, 0:size] = jnp.zeros((size, size), BF16)

    @pl.when(mode == 1)
    def _():
        out_ref[0:half] = factor[:, 0:size]
        out_ref[half:tile] = factor[:, size : 2 * size]

    @pl.when(mode == 2)
    def _():
        update = dot(factor[...], rows_ref[...])
        out_ref[0:half] = (slab_ref[0:half].astype(F32) - update[:, 0:size]).astype(BF16)
        out_ref[half:tile] = (slab_ref[half:tile].astype(F32) - update[:, size : 2 * size]).astype(BF16)

        @pl.when(top & (own == 1))
        def _():
            base = slab_ref[0:size].astype(F32) + added_ref[...]
            out_ref[0:size] = (base - update[0:size, 0:size]).astype(BF16)


def panel(flags, token, lower, weights, rows, added, slab, parts, old, start, tile):
    size = slab.shape[1]
    offset = start // tile
    spans, begin, operands = [], 0, []
    for hops in parts:
        end = begin + hops[0].shape[0] // tile
        spans.append((begin, end))
        begin = end
        operands += hops
    blocks = [
        SMEM,
        ANY,
        pl.BlockSpec((size, size), lambda i: (0, 0)),
        pl.BlockSpec(weights.shape, lambda i: (0, 0)),
        pl.BlockSpec(rows.shape, lambda i: (0, 0)),
        pl.BlockSpec((size, size), lambda i: (0, 0)),
        pl.BlockSpec((tile, size), lambda i: (i + offset, 0)),
    ] + [ANY] * len(operands)
    pieces = len(operands)
    operands = [flags, token, lower, weights, rows, added, slab] + operands
    aliases = {}
    if old is not None:
        aliases = {len(operands): 0}
        blocks.append(ANY)
        operands.append(old)
    return pl.pallas_call(
        functools.partial(panel_kernel, pieces=range(pieces), spans=spans, first=start == 0),
        grid=(begin,),
        in_specs=blocks,
        out_specs=[pl.BlockSpec((tile, size), lambda i: (i + offset, 0)), SMEM],
        out_shape=[jax.ShapeDtypeStruct(slab.shape, BF16), jax.ShapeDtypeStruct((1,), jnp.int32)],
        input_output_aliases=aliases,
        scratch_shapes=[
            pltpu.VMEM((2, tile, size), BF16),
            pltpu.VMEM((tile // 2, 2 * size), BF16),
            pltpu.SemaphoreType.DMA((2,)),
        ],
        compiler_params=pltpu.CompilerParams(vmem_limit_bytes=16 * 2**20),
        cost_estimate=LIGHT,
        name="panel",
    )(*operands)


def broadcast(value, axis, source):
    kept = jnp.where(lax.axis_index(axis) == source, value, 0).astype(value.dtype)
    return lax.psum(kept, axis)


def settings(*values):
    return jnp.stack([jnp.asarray(value).astype(jnp.int32) for value in values])


def holder_pairs(wide, narrow, distance):
    stride = wide // narrow
    found = []
    for n in range(narrow):
        for start in range(0, wide, 2 * distance):
            source = (n * stride) ^ start
            found.append((source * narrow + n, (source ^ distance) * narrow + n))
    return found


class Order:
    def __init__(self, token):
        self.token = token

    def after(self, value):
        value, self.token = lax.optimization_barrier((value, self.token))
        return value


def known_owner(owner, coarse_basis, material_ids, lame_table, coarse_ids, coarse_slab):
    narrow, wide = lax.axis_size("narrow"), lax.axis_size("wide")
    stride = wide // narrow
    wide_index, narrow_index = lax.axis_index("wide"), lax.axis_index("narrow")
    height, block = coarse_slab.shape
    own = wide_index == narrow_index * stride
    later = narrow_index > owner
    which = jnp.where(later, narrow_index - owner - 1, -1)
    mode = jnp.where(narrow_index == owner, 1, jnp.where(later, 2, 0))
    earlier = (wide_index % stride == 0) & (wide_index // stride < owner)
    kind = jnp.where(wide_index == owner * stride, 1, jnp.where(earlier, 2, 0))
    table = lame_table.astype(F32)
    hops = narrow - 1 - owner
    units, joined, plan = PLANS[hops]
    unit = height // sum(units)
    count = len(units)
    bounds, low = [], 0
    for number in units:
        bounds.append((low, low + number * unit))
        low += number * unit
    axes = ("wide", "narrow")

    def rows_of(number):
        low, high = bounds[number]
        return coarse_slab[low:high]

    def send(value, source, target):
        return lax.ppermute(value, "narrow", [(owner + source, owner + target)])

    order = Order(settings(mode))

    ways = [((n * stride) * narrow + owner, (n * stride) * narrow + n) for n in range(owner + 1, narrow)]
    moved = {}

    groups = [[w for w in range(wide) if w % stride == 0], [w for w in range(wide) if w % stride]]
    groups = [group for group in groups if group]
    member = jnp.where(wide_index % stride == 0, 0, 1)

    def within(group, pairs):
        return [(w * narrow + one, w * narrow + two) for w in group for one, two in pairs]

    def halo_of(group, message):
        return lax.ppermute(message, axes, within(group, [(i + 1, i) for i in range(narrow - 1)]))

    spans = [bounds[0], (bounds[joined[0]][0], bounds[joined[-1]][1]) if joined else bounds[1]]
    first, last, *begun = halo_message(table, material_ids, order.token, coarse_basis, coarse_slab, spans)
    first = order.after(first)
    halos = [halo_of(groups[0], first)]
    edge = (narrow_index == 0).astype(jnp.int32).reshape(1)
    inner = order.after(interior(edge, table, material_ids, coarse_basis, order.token))
    head = order.after(lax.ppermute(order.after(coarse_slab[:block]), axes, ways))
    halos[0] = order.after(halos[0])
    moved[0] = [send(order.after(begun[0]), 0, hops)]
    for group in groups[1:]:
        halos.append(halo_of(group, order.after(first)))

    def nearest(base, extent):
        return min(range(base, min(base + extent, narrow)), key=lambda n: abs(n - owner))

    def summed(parts, distance, group):
        total = parts[0] if len(parts) == 1 else parts[0] + parts[1]
        pairs = []
        for base in range(0, narrow - distance, 2 * distance):
            one, two = nearest(base, distance), nearest(base + distance, distance)
            pairs.append((two, one) if nearest(base, 2 * distance) == one else (one, two))
        return [total, lax.ppermute(total, axes, within(group, pairs))], 2 * distance

    def faces_of(number):
        flag = settings(member == number)
        return [order.after(face(flag, table, material_ids, last, halos[number], order.token, inner))]

    sums, reach = [faces_of(0)], [1]
    while reach[0] < narrow:
        sums[0], reach[0] = summed(sums[0], reach[0], groups[0])
    sums[0][1] = order.after(sums[0][1])
    distance, messages, left = wide // 2, [], plan.count("spread")
    result, prepared = None, None
    choice = (narrow_index - owner) % narrow
    flags = settings(mode, kind, own, which)
    for step in plan:
        if step[0] == "panel":
            if prepared is None:
                prepared = prepare(settings(choice, mode), order.token, head, summaries)
            weights, rows, lower = prepared
            begin, end = step[1:]
            parts = [moved[number][:: 1 if number else -1] for number in range(begin, end)]
            result, order.token = panel(
                flags, order.token, lower, weights, rows, added if begin == 0 else head, coarse_slab, parts, result, bounds[begin][0], 2 * unit
            )
        elif step == "sums":
            for place in range(1, narrow):
                galerkins[place] = order.after(galerkins[place])
            added, galerkin = added_of(settings(choice, mode, own), order.token, coarse_ids, galerkins, block)
            added = order.after(added)
        elif step == "next":
            if joined:
                whole = send(order.after(begun[1]), 0, 1)
            else:
                moved[1] = [send(order.after(begun[1]), 0, 1)]
                for number in range(2, count - 1):
                    moved[number] = [send(order.after(rows_of(number)), 0, 1)]
        elif step == "assemble":
            message = assemble(settings(mode, own), order.token, coarse_ids, coarse_slab, head, sums[0])
            message = order.after(message)
        elif step == "others":
            for number in range(1, len(groups)):
                halos[number] = order.after(halos[number])
                parts, far = summed(faces_of(number), 1, groups[number])
                sums.append(parts)
                reach.append(far)
        elif step == "more":
            for number in range(1, len(groups)):
                while reach[number] < narrow:
                    sums[number][1] = order.after(sums[number][1])
                    sums[number], reach[number] = summed(sums[number], reach[number], groups[number])
        elif step == "spread":
            left -= 1
            while distance:
                received = order.after(lax.ppermute(message, axes, holder_pairs(wide, narrow, distance)))
                messages = [message, received]
                if distance > 1:
                    message = message + received
                distance //= 2
                if left:
                    break
        elif step == "factor":
            summary, head, galerkin = factorize(settings(mode, member), order.token, messages, sums)
            summary = order.after(summary)
            ways = [[(owner, (owner + place) % narrow)] for place in range(1, narrow)]
            summaries = [summary] + [lax.ppermute(summary, "narrow", way) for way in ways]
        elif step == "summary":
            for place in range(1, narrow):
                summaries[place] = order.after(summaries[place])
            moved[count - 1] = [send(order.after(rows_of(count - 1)), 0, 1)]
            galerkin = order.after(galerkin)
            galerkins = [galerkin] + [lax.ppermute(galerkin, "narrow", way) for way in ways]
        else:
            number, hop = step
            if joined and step == (joined[0], 0):
                whole = order.after(whole)
                for part in joined:
                    low, high = (bound - bounds[joined[0]][0] for bound in bounds[part])
                    moved[part] = [whole[low:high]]
            moving = moved[number][hop] = order.after(moved[number][hop])
            if number == 0 and hop + 1 < hops:
                moved[number].append(send(moving, hops - hop, hops - hop - 1))
            elif number != 0 and hop + 1 < hops:
                moved[number].append(send(moving, hop + 1, hop + 2))
    return result, galerkin


def any_owner(owner, coarse_basis, material_ids, lame_table, coarse_ids, coarse_slab):
    narrow, wide = lax.axis_size("narrow"), lax.axis_size("wide")
    stride = wide // narrow
    wide_index, narrow_index = lax.axis_index("wide"), lax.axis_index("narrow")
    own = wide_index == narrow_index * stride
    later = narrow_index > owner
    which = jnp.where(later, 0, -1)
    mode = jnp.where(narrow_index == owner, 1, jnp.where(later, 2, 0))
    earlier = (wide_index % stride == 0) & (wide_index // stride < owner)
    kind = jnp.where(wide_index == owner * stride, 1, jnp.where(earlier, 2, 0))
    table = lame_table.astype(F32)
    column = broadcast(coarse_slab, "narrow", owner)
    first, last = halo_message(table, material_ids, table, coarse_basis, coarse_slab, ())
    halo = lax.ppermute(first, "narrow", [(i + 1, i) for i in range(narrow - 1)])
    edge = (narrow_index == 0).astype(jnp.int32).reshape(1)
    inner = interior(edge, table, material_ids, coarse_basis, first)
    partial = face(settings(1), table, material_ids, last, halo, first, inner)
    parts = [lax.psum(partial, "narrow")]
    message = assemble(settings(mode, own), first, coarse_ids, coarse_slab, column, parts)
    at_owner = (wide_index == owner * stride) & (narrow_index == owner)
    diagonal = lax.psum(jnp.where(at_owner, message, 0.0), ("wide", "narrow"))
    summary, _, galerkin = factorize(settings(1, 0), first, [diagonal], [parts])
    head = broadcast(message, "wide", narrow_index * stride)
    weights, rows, lower = prepare(settings(0, mode), settings(mode), head, [summary])
    added, galerkin = added_of(settings(0, mode, own), weights, coarse_ids, [galerkin], head.shape[0])
    flags = settings(mode, kind, own, which)
    tile = coarse_slab.shape[0] // 12
    result, _ = panel(flags, flags, lower, weights, rows, added, coarse_slab, [[column]], None, 0, tile)
    return result, galerkin


def on_device(coarse_basis, material_ids, lame_table, coarse_ids, coarse_slab, panel_owner):
    narrow, wide = lax.axis_size("narrow"), lax.axis_size("wide")
    arrays = (coarse_basis, material_ids, lame_table, coarse_ids, coarse_slab)
    owner = panel_owner[0]
    if narrow - 1 > len(PLANS) or wide & (wide - 1):
        return any_owner(owner, *arrays)
    branches = [functools.partial(known_owner, place) for place in range(narrow - 1)]
    return lax.switch(owner, branches, *arrays)


def solution(mesh):
    return jax.shard_map(
        on_device,
        mesh=mesh,
        in_specs=(
            P("wide", None, None, "narrow", None, None),
            P("wide", "narrow", None, None),
            P(),
            P("wide", None),
            P("wide", "narrow"),
            P(),
        ),
        out_specs=(P("wide", "narrow"), P("wide", None, None)),
        check_vma=False,
    )
```

profile of v0, /device:TPU:22, one launch (start us, length us, event | category | flops | bytes accessed | tf_op | source)
XLA Modules:
  0.0 138.3 jit_solution(1605483164182857910)
XLA Ops:
  1.3 136.8 %conditional.1 = (bf16[12288,128]{1,0:T(8,128)(2,1)}, f32[2,96,96]{2,1,0:T(8,128)}) conditional(s32[]{:T(128)} %bitcast.33, (bf16[2,16]{1,0:T(2,128)(2,1)}, s32[2,4,8,128]{3,2,1,0:T(8,128)}, bf16[2,96,3,4,8,128]{5,4,3,2,1,0:T(8,128)(2,1)}, bf16[12288,128]{1,0:T(8,128)(2,1)}, s32[2,96]{1,0:T(2,128)}) %tuple.115, ...), branch_computations={%region_0.1_spmd, %region_1.2_spmd, %region_2.3_spmd} | conditional | flops 69757 | bytes 88923216 | solution.py:815
  2.0 5.5 %halo_message.4 = (bf16[2,290,8,128]{3,2,1,0:T(8,128)(2,1)}, bf16[2,288,8,128]{3,2,1,0:T(8,128)(2,1)S(1)}, bf16[6144,128]{1,0:T(8,128)(2,1)}, bf16[3072,128]{1,0:T(8,128)(2,1)S(1)}) custom-call(f32[2,16]{1,0:T(2,128)S(1)} %convert_element_type.2.table_ref, s32[2,4,8,128]{3,2,1,0:T(8,128)} %get-tuple-element.125.ids_ref, s32[1]{0:T(128)} %bitcast.11.token_ref, ...), custom_call_target="tpu_custom_call" | custom-call | flops 1 | bytes 1 | tf_op jit(solution)/shard_map/cond/branch_1_fun/halo_message/pallas_call | solution.py:91
  7.5 0.9 copy-done.28
  8.4 2.5 %collective-permute-start.27 = (bf16[2,290,8,128]{3,2,1,0:T(8,128)(2,1)}, bf16[2,290,8,128]{3,2,1,0:T(8,128)(2,1)S(1)}, u32[]{:S(2)}, u32[]{:S(2)}) collective-permute-start(bf16[2,290,8,128]{3,2,1,0:T(8,128)(2,1)} %get-tuple-element.156), channel_id=1, source_target_pairs={{1,0},{2,1},{3,2},{9,8},{10,9},{11,10},{17,16},{18,17},{19,18},{25... | collective-permute-start | bytes 3563528 | tf_op jit(solution)/shard_map/cond/branch_1_fun/ppermute | solution.py:668
  11.0 10.7 %interior.4.inner_ref = f32[2,96,96]{2,1,0:T(8,128)S(1)} custom-call(s32[1]{0:T(128)} %bitcast.18.edge_ref, f32[2,16]{1,0:T(2,128)S(1)} %convert_element_type.2.table_ref, s32[2,4,8,128]{3,2,1,0:T(8,128)S(1)} %copy-done.34, bf16[2,96,3,4,8,128]{5,4,3,2,1,0:T(8,128)(2,1)} %get-tuple-element.126.basis_ref, s32[1]{0:T(128)} %bitcast.11.token_ref), custom_call_target="tpu_custom_call" | custom-call | flops 1 | bytes 1 | tf_op jit(solution)/shard_map/cond/branch_1_fun/interior/pallas_call | solution.py:187
  21.7 0.8 slice.22
  23.1 3.6 %collective-permute-done.27.halo_ref = bf16[2,290,8,128]{3,2,1,0:T(8,128)(2,1)S(1)} collective-permute-done((bf16[2,290,8,128]{3,2,1,0:T(8,128)(2,1)}, bf16[2,290,8,128]{3,2,1,0:T(8,128)(2,1)S(1)}, u32[]{:S(2)}, u32[]{:S(2)}) %collective-permute-start.27) | collective-permute-done | bytes 1187872 | tf_op jit(solution)/shard_map/cond/branch_1_fun/ppermute | solution.py:668
  26.8 1.0 copy-done
  27.8 0.7 collective-permute-start.32
  28.6 1.7 %collective-permute-start.35 = (bf16[2,290,8,128]{3,2,1,0:T(8,128)(2,1)}, bf16[2,290,8,128]{3,2,1,0:T(8,128)(2,1)}, u32[]{:S(2)}, u32[]{:S(2)}) collective-permute-start(bf16[2,290,8,128]{3,2,1,0:T(8,128)(2,1)} %get-tuple-element.156), channel_id=1, source_target_pairs={{5,4},{6,5},{7,6},{13,12},{14,13},{15,14},{21,20},{22,21},{23,22},... | collective-permute-start | bytes 3563528 | tf_op jit(solution)/shard_map/cond/branch_1_fun/ppermute | solution.py:668
  30.3 1.3 copy-done.1
  31.6 4.5 %face.8 = f32[2,96,96]{2,1,0:T(8,128)S(1)} custom-call(s32[1]{0:T(128)} %bitcast.17.flags_ref, f32[2,16]{1,0:T(2,128)S(1)} %convert_element_type.2.table_ref, s32[2,4,8,128]{3,2,1,0:T(8,128)S(1)} %copy-done.34, bf16[2,288,8,128]{3,2,1,0:T(8,128)(2,1)S(1)} %get-tuple-element.129.last_ref, bf16[2,290,8,128]{3,2,1,0:T(8,128)(2,1)S(1)} %copy-done.1, ...), custom_call_target="tpu_custom_call" | custom-call | flops 1 | bytes 1 | tf_op jit(solution)/shard_map/cond/branch_1_fun/face/pallas_call | solution.py:265
  36.1 1.3 collective-permute-start.29
  37.4 0.8 copy.15.column_ids_ref
  38.2 6.7 %collective-permute-done.29 = f32[2,96,96]{2,1,0:T(8,128)S(1)} collective-permute-done((f32[2,96,96]{2,1,0:T(8,128)S(1)}, f32[2,96,96]{2,1,0:T(8,128)S(1)}, u32[]{:S(2)}, u32[]{:S(2)}) %collective-permute-start.29) | collective-permute-done | bytes 73760 | tf_op jit(solution)/shard_map/cond/branch_1_fun/ppermute | solution.py:691
  44.8 6.7 %collective-permute-start.30 = (f32[2,96,96]{2,1,0:T(8,128)S(1)}, f32[2,96,96]{2,1,0:T(8,128)S(1)}, u32[]{:S(2)}, u32[]{:S(2)}) collective-permute-start(f32[2,96,96]{2,1,0:T(8,128)S(1)} %add.60.rest_0_.refs_2_), channel_id=1, source_target_pairs={{2,1},{10,9},{18,17},{26,25}} | collective-permute-start | bytes 221192 | tf_op jit(solution)/shard_map/cond/branch_1_fun/ppermute | solution.py:691
  52.2 1.6 %collective-permute-done.30.rest_1_.refs_3_ = f32[2,96,96]{2,1,0:T(8,128)S(1)} collective-permute-done((f32[2,96,96]{2,1,0:T(8,128)S(1)}, f32[2,96,96]{2,1,0:T(8,128)S(1)}, u32[]{:S(2)}, u32[]{:S(2)}) %collective-permute-start.30) | collective-permute-done | bytes 73760 | tf_op jit(solution)/shard_map/cond/branch_1_fun/ppermute | solution.py:691
  54.4 1.7 %assemble.4 = f32[128,128]{1,0:T(8,128)} custom-call(s32[2]{0:T(128)} %pad_add_fusion.8.flags_ref, s32[1]{0:T(128)} %bitcast.11.token_ref, s32[2,96,1]{2,1,0:T(8,128)} %copy.15.column_ids_ref, s32[2,1,96]{2,1,0:T(1,128)S(1)} %bitcast.38, bf16[12288,128]{1,0:T(8,128)(2,1)} %get-tuple-element.127.slab_ref, bf16[128,128]{1,0:T(8,128)(2,1)} %copy-done.66, ...), custom_call_target="tpu_custom_call" | custom-call | flops 1 | bytes 1 | tf_op jit(solution)/shard_map/cond/branch_1_fun/assemble/pallas_call | solution.py:322
  56.1 1.3 collective-permute-start.31
  58.1 1.9 %slice.23 = bf16[2048,128]{1,0:T(8,128)(2,1)} slice(bf16[12288,128]{1,0:T(8,128)(2,1)} %get-tuple-element.127.slab_ref), slice={[9216:11264], [0:128]} | slice | bytes 1048576 | tf_op jit(solution)/shard_map/cond/branch_1_fun/slice | solution.py:650
  59.9 0.9 add.61
  60.8 1.3 collective-permute-start.34
  62.7 0.7 collective-permute-start.37
  63.4 3.6 %collective-permute-done.34 = f32[128,128]{1,0:T(8,128)S(1)} collective-permute-done((f32[128,128]{1,0:T(8,128)S(1)}, f32[128,128]{1,0:T(8,128)S(1)}, u32[]{:S(2)}, u32[]{:S(2)}) %collective-permute-start.34) | collective-permute-done | bytes 65568 | tf_op jit(solution)/shard_map/cond/branch_1_fun/ppermute | solution.py:744
  67.0 1.3 collective-permute-start.36
  68.3 0.9 collective-permute-done.36.refs_1_
  69.2 1.3 collective-permute-start.48
  70.4 1.3 collective-permute-start.42
  71.7 8.3 %collective-permute-done.31.rest_0_ = bf16[3072,128]{1,0:T(8,128)(2,1)} collective-permute-done((bf16[3072,128]{1,0:T(8,128)(2,1)}, bf16[3072,128]{1,0:T(8,128)(2,1)}, u32[]{:S(2)}, u32[]{:S(2)}) %collective-permute-start.31) | collective-permute-done | bytes 786464 | tf_op jit(solution)/shard_map/cond/branch_1_fun/ppermute | solution.py:653
  80.1 1.3 collective-permute-start.47
  83.4 1.8 %factorize.4 = (bf16[384,128]{1,0:T(8,128)(2,1)}, f32[128,128]{1,0:T(8,128)}, f32[2,96,96]{2,1,0:T(8,128)}) custom-call(s32[2]{0:T(128)} %pad_add_fusion.7.flags_ref, s32[1]{0:T(128)} %bitcast.11.token_ref, f32[128,128]{1,0:T(8,128)} %copy-done.46, f32[128,128]{1,0:T(8,128)} %copy-done.62, f32[2,96,96]{2,1,0:T(8,128)} %copy-done.36, ...), custom_call_target="tpu_custom_call" | custom-call | flops 1 | bytes 1 | tf_op jit(solution)/shard_map/cond/branch_1_fun/factorize/pallas_call | solution.py:394
  85.2 1.3 collective-permute-start.41
  87.2 3.1 %collective-permute-done.42.rest_0_ = bf16[2048,128]{1,0:T(8,128)(2,1)S(1)} collective-permute-done((bf16[2048,128]{1,0:T(8,128)(2,1)}, bf16[2048,128]{1,0:T(8,128)(2,1)S(1)}, u32[]{:S(2)}, u32[]{:S(2)}) %collective-permute-start.42) | collective-permute-done | bytes 524320 | tf_op jit(solution)/shard_map/cond/branch_1_fun/ppermute | solution.py:653
  90.9 1.7 %slice.24 = bf16[1024,128]{1,0:T(8,128)(2,1)} slice(bf16[12288,128]{1,0:T(8,128)(2,1)} %get-tuple-element.127.slab_ref), slice={[11264:12288], [0:128]} | slice | bytes 524288 | tf_op jit(solution)/shard_map/cond/branch_1_fun/slice | solution.py:650
  93.7 1.3 collective-permute-start.46
  95.0 6.5 %collective-permute-start.49 = (bf16[2048,128]{1,0:T(8,128)(2,1)S(1)}, bf16[2048,128]{1,0:T(8,128)(2,1)}, u32[]{:S(2)}, u32[]{:S(2)}) collective-permute-start(bf16[2048,128]{1,0:T(8,128)(2,1)S(1)} %collective-permute-done.42.rest_0_), channel_id=1, source_target_pairs={{2,3},{6,7},{10,11},{14,15},{18,19},{22,23},{26,27},{30,31}} | collective-permute-start | bytes 1572872 | tf_op jit(solution)/shard_map/cond/branch_1_fun/ppermute | solution.py:653
  101.6 0.8 copy-done.7
  102.5 0.9 copy-done.16
  103.4 0.9 copy-done.22
  104.3 1.0 prepare.4
  105.3 4.9 %panel.11 = (bf16[12288,128]{1,0:T(8,128)(2,1)}, s32[1]{0:T(128)}) custom-call(s32[4]{0:T(128)S(1)} %pad_add_fusion.5.flags_ref, s32[1]{0:T(128)} %bitcast.11.token_ref, bf16[128,128]{1,0:T(8,128)(2,1)S(1)} %get-tuple-element.187.lower_ref, bf16[512,256]{1,0:T(8,128)(2,1)S(1)} %get-tuple-element.188.weights_ref, ...), custom_call_target="tpu_custom_call" | custom-call | flops 1 | bytes 1 | tf_op jit(solution)/shard_map/cond/branch_1_fun/panel/pallas_call | solution.py:580
  110.2 1.3 collective-permute-start.50
  111.5 1.3 collective-permute-start.45
  113.5 5.5 %collective-permute-done.45.rest_1_ = f32[2,96,96]{2,1,0:T(8,128)S(1)} collective-permute-done((f32[2,96,96]{2,1,0:T(8,128)S(1)}, f32[2,96,96]{2,1,0:T(8,128)S(1)}, u32[]{:S(2)}, u32[]{:S(2)}) %collective-permute-start.45) | collective-permute-done | bytes 73760 | tf_op jit(solution)/shard_map/cond/branch_1_fun/ppermute | solution.py:761
  121.6 2.4 %added.4 = (f32[128,128]{1,0:T(8,128)}, f32[2,96,96]{2,1,0:T(8,128)}) custom-call(s32[3]{0:T(128)} %pad_add_fusion.6.flags_ref, s32[1]{0:T(128)} %get-tuple-element.200.token_ref, s32[2,96,1]{2,1,0:T(8,128)} %copy.15.column_ids_ref, s32[2,1,96]{2,1,0:T(1,128)S(1)} %bitcast.39, f32[2,96,96]{2,1,0:T(8,128)} %get-tuple-element.180.rest_0_, ...), custom_call_target="tpu_custom_call" | custom-call | flops 1 | bytes 1 | tf_op jit(solution)/shard_map/cond/branch_1_fun/added/pallas_call | solution.py:472
  124.1 0.8 copy-done.25
  124.9 8.5 %panel.12 = (bf16[12288,128]{1,0:T(8,128)(2,1)}, s32[1]{0:T(128)}) custom-call(s32[4]{0:T(128)S(1)} %pad_add_fusion.5.flags_ref, s32[1]{0:T(128)} %get-tuple-element.200.token_ref, bf16[128,128]{1,0:T(8,128)(2,1)S(1)} %get-tuple-element.187.lower_ref, bf16[512,256]{1,0:T(8,128)(2,1)S(1)} %get-tuple-element.188.weights_ref, ...), custom_call_target="tpu_custom_call", output_to_operand_aliasing={{0}: (9, {})} | custom-call | flops 1 | bytes 1 | tf_op jit(solution)/shard_map/cond/branch_1_fun/panel/pallas_call | solution.py:580
  133.4 4.2 %panel.13 = (bf16[12288,128]{1,0:T(8,128)(2,1)}, s32[1]{0:T(128)}) custom-call(s32[4]{0:T(128)S(1)} %pad_add_fusion.5.flags_ref, s32[1]{0:T(128)} %get-tuple-element.204.token_ref, bf16[128,128]{1,0:T(8,128)(2,1)S(1)} %get-tuple-element.187.lower_ref, bf16[512,256]{1,0:T(8,128)(2,1)S(1)} %get-tuple-element.188.weights_ref, ...), custom_call_target="tpu_custom_call", output_to_operand_aliasing={{0}: (11, {})} | custom-call | flops 1 | bytes 1 | tf_op jit(solution)/shard_map/cond/branch_1_fun/panel/pallas_call | solution.py:580
  (72 shorter events, 11.7 us)
Async XLA Ops:
  2.0 9.0 %copy-start.34 = (s32[2,4,8,128]{3,2,1,0:T(8,128)S(1)}, s32[2,4,8,128]{3,2,1,0:T(8,128)}, u32[]{:S(2)}) copy-start(s32[2,4,8,128]{3,2,1,0:T(8,128)} %get-tuple-element.125.ids_ref) | copy-start | bytes 98308 | tf_op jit(solution)/shard_map/cond
  7.5 0.9 copy-start.28
  8.4 18.4 %collective-permute-start.27 = (bf16[2,290,8,128]{3,2,1,0:T(8,128)(2,1)}, bf16[2,290,8,128]{3,2,1,0:T(8,128)(2,1)S(1)}, u32[]{:S(2)}, u32[]{:S(2)}) collective-permute-start(bf16[2,290,8,128]{3,2,1,0:T(8,128)(2,1)} %get-tuple-element.156), channel_id=1, source_target_pairs={{1,0},{2,1},{3,2},{9,8},{10,9},{11,10},{17,16},{18,17},{19,18},{25... | collective-permute-start | bytes 3563528 | tf_op jit(solution)/shard_map/cond/branch_1_fun/ppermute | solution.py:668
  21.7 15.7 %copy-start.60 = (s32[2,96]{1,0:T(2,128)S(1)}, s32[2,96]{1,0:T(2,128)}, u32[]{:S(2)}) copy-start(s32[2,96]{1,0:T(2,128)} %get-tuple-element.146) | copy-start | bytes 2308 | tf_op jit(solution)/shard_map/cond
  22.5 0.7 collective-permute-start.28
  23.1 30.6 %copy-start.66 = (bf16[128,128]{1,0:T(8,128)(2,1)}, bf16[128,128]{1,0:T(8,128)(2,1)S(1)}, u32[]{:S(2)}) copy-start(bf16[128,128]{1,0:T(8,128)(2,1)S(1)} %collective-permute-done.28.head_ref) | copy-start | bytes 98308 | tf_op jit(solution)/shard_map/cond
  26.8 1.0 copy-start
  27.8 41.3 %collective-permute-start.32 = (bf16[6144,128]{1,0:T(8,128)(2,1)}, bf16[6144,128]{1,0:T(8,128)(2,1)S(1)}, u32[]{:S(2)}, u32[]{:S(2)}) collective-permute-start(bf16[6144,128]{1,0:T(8,128)(2,1)} %get-tuple-element.151), channel_id=1, source_target_pairs={{1,3},{5,7},{9,11},{13,15},{17,19},{21,23},{25,27},{29,31}} | collective-permute-start | bytes 4718600 | tf_op jit(solution)/shard_map/cond/branch_1_fun/ppermute | solution.py:653
  28.6 33.5 %collective-permute-start.35 = (bf16[2,290,8,128]{3,2,1,0:T(8,128)(2,1)}, bf16[2,290,8,128]{3,2,1,0:T(8,128)(2,1)}, u32[]{:S(2)}, u32[]{:S(2)}) collective-permute-start(bf16[2,290,8,128]{3,2,1,0:T(8,128)(2,1)} %get-tuple-element.156), channel_id=1, source_target_pairs={{5,4},{6,5},{7,6},{13,12},{14,13},{15,14},{21,20},{22,21},{23,22},... | collective-permute-start | bytes 3563528 | tf_op jit(solution)/shard_map/cond/branch_1_fun/ppermute | solution.py:668
  30.3 1.3 copy-start.1
  36.1 8.8 %collective-permute-start.29 = (f32[2,96,96]{2,1,0:T(8,128)S(1)}, f32[2,96,96]{2,1,0:T(8,128)S(1)}, u32[]{:S(2)}, u32[]{:S(2)}) collective-permute-start(f32[2,96,96]{2,1,0:T(8,128)S(1)} %face.8), channel_id=1, source_target_pairs={{0,1},{3,2},{8,9},{11,10},{16,17},{19,18},{24,25},{27,26}} | collective-permute-start | bytes 221192 | tf_op jit(solution)/shard_map/cond/branch_1_fun/ppermute | solution.py:691
  44.8 8.9 %copy-start.36 = (f32[2,96,96]{2,1,0:T(8,128)}, f32[2,96,96]{2,1,0:T(8,128)S(1)}, u32[]{:S(2)}) copy-start(f32[2,96,96]{2,1,0:T(8,128)S(1)} %add.60.rest_0_.refs_2_) | copy-start | bytes 221188 | tf_op jit(solution)/shard_map/cond
  44.8 8.9 %collective-permute-start.30 = (f32[2,96,96]{2,1,0:T(8,128)S(1)}, f32[2,96,96]{2,1,0:T(8,128)S(1)}, u32[]{:S(2)}, u32[]{:S(2)}) collective-permute-start(f32[2,96,96]{2,1,0:T(8,128)S(1)} %add.60.rest_0_.refs_2_), channel_id=1, source_target_pairs={{2,1},{10,9},{18,17},{26,25}} | collective-permute-start | bytes 221192 | tf_op jit(solution)/shard_map/cond/branch_1_fun/ppermute | solution.py:691
  53.8 0.7 copy-start.39
  56.1 24.0 %collective-permute-start.31 = (bf16[3072,128]{1,0:T(8,128)(2,1)}, bf16[3072,128]{1,0:T(8,128)(2,1)}, u32[]{:S(2)}, u32[]{:S(2)}) collective-permute-start(bf16[3072,128]{1,0:T(8,128)(2,1)} %copy-done.28), channel_id=1, source_target_pairs={{1,2},{5,6},{9,10},{13,14},{17,18},{21,22},{25,26},{29,30}} | collective-permute-start | bytes 2359304 | tf_op jit(solution)/shard_map/cond/branch_1_fun/ppermute | solution.py:653
  57.4 2.6 %collective-permute-start.33 = (f32[128,128]{1,0:T(8,128)}, f32[128,128]{1,0:T(8,128)S(1)}, u32[]{:S(2)}, u32[]{:S(2)}) collective-permute-start(f32[128,128]{1,0:T(8,128)} %assemble.4), channel_id=1, source_target_pairs={{0,16},{9,25},{18,2},{27,11}} | collective-permute-start | bytes 196616 | tf_op jit(solution)/shard_map/cond/branch_1_fun/ppermute | solution.py:744
  60.8 6.2 %collective-permute-start.34 = (f32[128,128]{1,0:T(8,128)S(1)}, f32[128,128]{1,0:T(8,128)S(1)}, u32[]{:S(2)}, u32[]{:S(2)}) collective-permute-start(f32[128,128]{1,0:T(8,128)S(1)} %add.61), channel_id=1, source_target_pairs={{0,8},{16,24},{9,1},{25,17},{18,26},{2,10},{27,19},{11,3}} | collective-permute-start | bytes 196616 | tf_op jit(solution)/shard_map/cond/branch_1_fun/ppermute | solution.py:744
  62.7 5.6 %collective-permute-start.37 = (f32[2,96,96]{2,1,0:T(8,128)S(1)}, f32[2,96,96]{2,1,0:T(8,128)S(1)}, u32[]{:S(2)}, u32[]{:S(2)}) collective-permute-start(f32[2,96,96]{2,1,0:T(8,128)S(1)} %face.9), channel_id=1, source_target_pairs={{4,5},{7,6},{12,13},{15,14},{20,21},{23,22},{28,29},{31,30}} | collective-permute-start | bytes 221192 | tf_op jit(solution)/shard_map/cond/branch_1_fun/ppermute | solution.py:691
  67.0 15.8 %copy-start.46 = (f32[128,128]{1,0:T(8,128)}, f32[128,128]{1,0:T(8,128)S(1)}, u32[]{:S(2)}) copy-start(f32[128,128]{1,0:T(8,128)S(1)} %add.62.refs_0_) | copy-start | bytes 196612 | tf_op jit(solution)/shard_map/cond
  67.0 2.2 %collective-permute-start.36 = (f32[128,128]{1,0:T(8,128)S(1)}, f32[128,128]{1,0:T(8,128)S(1)}, u32[]{:S(2)}, u32[]{:S(2)}) collective-permute-start(f32[128,128]{1,0:T(8,128)S(1)} %add.62.refs_0_), channel_id=1, source_target_pairs={{0,4},{8,12},{16,20},{24,28},{9,13},{1,5},{25,29},{17,21},{18,22},... | collective-permute-start | bytes 196616 | tf_op jit(solution)/shard_map/cond/branch_1_fun/ppermute | solution.py:744
  69.2 13.6 %copy-start.62 = (f32[128,128]{1,0:T(8,128)}, f32[128,128]{1,0:T(8,128)S(1)}, u32[]{:S(2)}) copy-start(f32[128,128]{1,0:T(8,128)S(1)} %collective-permute-done.36.refs_1_) | copy-start | bytes 196612 | tf_op jit(solution)/shard_map/cond
  69.2 54.9 %collective-permute-start.48 = (bf16[6144,128]{1,0:T(8,128)(2,1)S(1)}, bf16[6144,128]{1,0:T(8,128)(2,1)}, u32[]{:S(2)}, u32[]{:S(2)}) collective-permute-start(bf16[6144,128]{1,0:T(8,128)(2,1)S(1)} %collective-permute-done.32.rest_1_), channel_id=1, source_target_pairs={{3,2},{7,6},{11,10},{15,14},{19,18},{23,22},{27,26},{31,30}} | collective-permute-start | bytes 4718600 | tf_op jit(solution)/shard_map/cond/branch_1_fun/ppermute | solution.py:653
  70.4 19.8 %collective-permute-start.42 = (bf16[2048,128]{1,0:T(8,128)(2,1)}, bf16[2048,128]{1,0:T(8,128)(2,1)S(1)}, u32[]{:S(2)}, u32[]{:S(2)}) collective-permute-start(bf16[2048,128]{1,0:T(8,128)(2,1)} %slice.23), channel_id=1, source_target_pairs={{1,2},{5,6},{9,10},{13,14},{17,18},{21,22},{25,26},{29,30}} | collective-permute-start | bytes 1572872 | tf_op jit(solution)/shard_map/cond/branch_1_fun/ppermute | solution.py:653
  80.1 25.2 %collective-permute-start.47 = (bf16[3072,128]{1,0:T(8,128)(2,1)}, bf16[3072,128]{1,0:T(8,128)(2,1)S(1)}, u32[]{:S(2)}, u32[]{:S(2)}) collective-permute-start(bf16[3072,128]{1,0:T(8,128)(2,1)} %collective-permute-done.31.rest_0_), channel_id=1, source_target_pairs={{2,3},{6,7},{10,11},{14,15},{18,19},{22,23},{26,27},{30,31}} | collective-permute-start | bytes 2359304 | tf_op jit(solution)/shard_map/cond/branch_1_fun/ppermute | solution.py:653
  81.4 1.3 copy-start.44
  81.4 1.3 collective-permute-start.38
  82.7 0.7 copy-start.51
  85.2 7.8 %collective-permute-start.41 = (bf16[384,128]{1,0:T(8,128)(2,1)}, bf16[384,128]{1,0:T(8,128)(2,1)S(1)}, u32[]{:S(2)}, u32[]{:S(2)}) collective-permute-start(bf16[384,128]{1,0:T(8,128)(2,1)} %get-tuple-element.172.rest_0_), channel_id=1, source_target_pairs={{1,2},{5,6},{9,10},{13,14},{17,18},{21,22},{25,26},{29,30}} | collective-permute-start | bytes 294920 | tf_op jit(solution)/shard_map/cond/branch_1_fun/ppermute | solution.py:755
  86.5 6.6 %collective-permute-start.40 = (bf16[384,128]{1,0:T(8,128)(2,1)}, bf16[384,128]{1,0:T(8,128)(2,1)S(1)}, u32[]{:S(2)}, u32[]{:S(2)}) collective-permute-start(bf16[384,128]{1,0:T(8,128)(2,1)} %get-tuple-element.172.rest_0_), channel_id=1, source_target_pairs={{1,3},{5,7},{9,11},{13,15},{17,19},{21,23},{25,27},{29,31}} | collective-permute-start | bytes 294920 | tf_op jit(solution)/shard_map/cond/branch_1_fun/ppermute | solution.py:755
  90.3 2.8 %collective-permute-start.39 = (bf16[384,128]{1,0:T(8,128)(2,1)}, bf16[384,128]{1,0:T(8,128)(2,1)S(1)}, u32[]{:S(2)}, u32[]{:S(2)}) collective-permute-start(bf16[384,128]{1,0:T(8,128)(2,1)} %get-tuple-element.172.rest_0_), channel_id=1, source_target_pairs={{1,0},{5,4},{9,8},{13,12},{17,16},{21,20},{25,24},{29,28}} | collective-permute-start | bytes 294920 | tf_op jit(solution)/shard_map/cond/branch_1_fun/ppermute | solution.py:755
  93.1 0.6 copy-start.21
  93.7 16.5 %collective-permute-start.46 = (bf16[1024,128]{1,0:T(8,128)(2,1)}, bf16[1024,128]{1,0:T(8,128)(2,1)}, u32[]{:S(2)}, u32[]{:S(2)}) collective-permute-start(bf16[1024,128]{1,0:T(8,128)(2,1)} %slice.24), channel_id=1, source_target_pairs={{1,2},{5,6},{9,10},{13,14},{17,18},{21,22},{25,26},{29,30}} | collective-permute-start | bytes 786440 | tf_op jit(solution)/shard_map/cond/branch_1_fun/ppermute | solution.py:653
  95.0 38.4 %collective-permute-start.49 = (bf16[2048,128]{1,0:T(8,128)(2,1)S(1)}, bf16[2048,128]{1,0:T(8,128)(2,1)}, u32[]{:S(2)}, u32[]{:S(2)}) collective-permute-start(bf16[2048,128]{1,0:T(8,128)(2,1)S(1)} %collective-permute-done.42.rest_0_), channel_id=1, source_target_pairs={{2,3},{6,7},{10,11},{14,15},{18,19},{22,23},{26,27},{30,31}} | collective-permute-start | bytes 1572872 | tf_op jit(solution)/shard_map/cond/branch_1_fun/ppermute | solution.py:653
  101.6 0.8 copy-start.7
  102.5 0.9 copy-start.16
  103.4 0.9 copy-start.22
  105.3 6.2 %copy-start.53 = (f32[2,96,96]{2,1,0:T(8,128)S(1)}, f32[2,96,96]{2,1,0:T(8,128)}, u32[]{:S(2)}) copy-start(f32[2,96,96]{2,1,0:T(8,128)} %get-tuple-element.180.rest_0_) | copy-start | bytes 221188 | tf_op jit(solution)/shard_map/cond
  110.2 23.2 %collective-permute-start.50 = (bf16[1024,128]{1,0:T(8,128)(2,1)}, bf16[1024,128]{1,0:T(8,128)(2,1)S(1)}, u32[]{:S(2)}, u32[]{:S(2)}) collective-permute-start(bf16[1024,128]{1,0:T(8,128)(2,1)} %collective-permute-done.46.rest_2_), channel_id=1, source_target_pairs={{2,3},{6,7},{10,11},{14,15},{18,19},{22,23},{26,27},{30,31}} | collective-permute-start | bytes 786440 | tf_op jit(solution)/shard_map/cond/branch_1_fun/ppermute | solution.py:653
  111.5 7.5 %collective-permute-start.45 = (f32[2,96,96]{2,1,0:T(8,128)S(1)}, f32[2,96,96]{2,1,0:T(8,128)S(1)}, u32[]{:S(2)}, u32[]{:S(2)}) collective-permute-start(f32[2,96,96]{2,1,0:T(8,128)S(1)} %copy-done.53), channel_id=1, source_target_pairs={{1,2},{5,6},{9,10},{13,14},{17,18},{21,22},{25,26},{29,30}} | collective-permute-start | bytes 221192 | tf_op jit(solution)/shard_map/cond/branch_1_fun/ppermute | solution.py:761
  112.8 7.5 %collective-permute-start.44 = (f32[2,96,96]{2,1,0:T(8,128)S(1)}, f32[2,96,96]{2,1,0:T(8,128)S(1)}, u32[]{:S(2)}, u32[]{:S(2)}) collective-permute-start(f32[2,96,96]{2,1,0:T(8,128)S(1)} %copy-done.53), channel_id=1, source_target_pairs={{1,3},{5,7},{9,11},{13,15},{17,19},{21,23},{25,27},{29,31}} | collective-permute-start | bytes 221192 | tf_op jit(solution)/shard_map/cond/branch_1_fun/ppermute | solution.py:761
  119.0 1.3 copy-start.55
  119.0 1.3 collective-permute-start.43
  120.4 0.7 copy-start.57
  121.0 0.6 copy-start.58
  124.1 0.8 copy-start.25
  124.9 8.5 %copy-start.8 = (f32[128,128]{1,0:T(8,128)S(1)}, f32[128,128]{1,0:T(8,128)}, u32[]{:S(2)}) copy-start(f32[128,128]{1,0:T(8,128)} %get-tuple-element.183.head_ref.added_ref) | copy-start | bytes 196612 | tf_op jit(solution)/shard_map/cond
  124.9 8.5 %copy-start.30 = (bf16[12288,128]{1,0:T(8,128)(2,1)S(1)}, bf16[12288,128]{1,0:T(8,128)(2,1)}, u32[]{:S(2)}) copy-start(bf16[12288,128]{1,0:T(8,128)(2,1)} %get-tuple-element.127.slab_ref) | copy-start | bytes 9437188 | tf_op jit(solution)/shard_map/cond
where the time goes:
time: 140 us; the launch traced here: 138 us
  Pallas kernels  45.8 us (33%)
  starting transfers between devices  37.7 us (27%)
  waiting for transfers between devices  33.8 us (24%)
  local copies, waits for them, and re-layouts  15 us (11%)
  other arithmetic  3.55 us (3%)
  between operations  1.48 us (1%)
    pallas_call x3, Pallas kernels, panel(): pl.pallas_call(functools.partial(panel_kernel, pieces=range(pieces), span...  17.5 us
    ppermute x8, starting transfers between devices, send(): return lax.ppermute(value, 'narrow', [(owner + source, owner + target)])  15 us
    ppermute x8, waiting for transfers between devices, send(): return lax.ppermute(value, 'narrow', [(owner + source, owner + target)])  11.4 us
    pallas_call x1, Pallas kernels, interior(): pl.pallas_call(interior_kernel, grid=(subs, comps), in_specs=[SMEM, SMEM,...  10.7 us
    cond x46, local copies, waits for them, and re-layouts  9.91 us
    ppermute x4, starting transfers between devices, summed(): lax.ppermute(total, axes, within(group, pairs))  9.35 us
    ppermute x4, waiting for transfers between devices, summed(): lax.ppermute(total, axes, within(group, pairs))  8.27 us
    ppermute x3, waiting for transfers between devices, known_owner(): lax.ppermute(galerkin, 'narrow', way)  5.54 us
  transfers between devices with their start and end apart: 24, of which 9 were waited for; matrix products, arithmetic and copies ran while one was open for 6% of the time, Pallas kernels for 26%

commit v1 on v0

--- a/solution.py
+++ b/solution.py
@@ -16,7 +16,8 @@
 PLANS = {
     1: (
         (12, 6, 6),
-        (),
+        False,
+        True,
         (
             "assemble", "next", "spread", "others", "spread", "more", "spread", (0, 0), "factor", "summary",
             "sums", ("panel", 0, 2), ("panel", 2, 3),
@@ -24,18 +25,20 @@
     ),
     2: (
         (12, 6, 4, 2),
-        (),
+        False,
+        True,
         (
             "assemble", "next", "spread", "others", "spread", "more", "spread", (0, 0), (1, 0), "factor", (2, 0),
-            "summary", ("panel", 1, 2), (3, 0), "sums", ("panel", 0, 1), ("panel", 2, 4),
+            "summary", "sums", ("panel", 1, 2), (3, 0), ("panel", 0, 1), ("panel", 2, 4),
         ),
     ),
     3: (
-        (12, 6, 4, 2),
-        (1, 2),
+        (12, 6, 6),
+        True,
+        False,
         (
             "assemble", "next", "spread", "others", "spread", "more", "spread", (0, 0), "factor", (1, 0), "summary",
-            (0, 1), (1, 1), (2, 0), (2, 1), ("panel", 1, 2), (3, 0), (3, 1), "sums", ("panel", 0, 1), ("panel", 2, 4),
+            (0, 1), (1, 1), (2, 0), ("panel", 1, 2), (2, 1), "sums", ("panel", 0, 1), ("panel", 2, 3),
         ),
     ),
 }
@@ -636,7 +639,7 @@
     kind = jnp.where(wide_index == owner * stride, 1, jnp.where(earlier, 2, 0))
     table = lame_table.astype(F32)
     hops = narrow - 1 - owner
-    units, joined, plan = PLANS[hops]
+    units, joined, waits, plan = PLANS[hops]
     unit = height // sum(units)
     count = len(units)
     bounds, low = [], 0
@@ -667,7 +670,7 @@
     def halo_of(group, message):
         return lax.ppermute(message, axes, within(group, [(i + 1, i) for i in range(narrow - 1)]))
 
-    spans = [bounds[0], (bounds[joined[0]][0], bounds[joined[-1]][1]) if joined else bounds[1]]
+    spans = [bounds[0], (bounds[1][0], height) if joined else bounds[1]]
     first, last, *begun = halo_message(table, material_ids, order.token, coarse_basis, coarse_slab, spans)
     first = order.after(first)
     halos = [halo_of(groups[0], first)]
@@ -722,7 +725,7 @@
                 whole = send(order.after(begun[1]), 0, 1)
             else:
                 moved[1] = [send(order.after(begun[1]), 0, 1)]
-                for number in range(2, count - 1):
+                for number in range(2, count - waits):
                     moved[number] = [send(order.after(rows_of(number)), 0, 1)]
         elif step == "assemble":
             message = assemble(settings(mode, own), order.token, coarse_ids, coarse_slab, head, sums[0])
@@ -756,15 +759,16 @@
         elif step == "summary":
             for place in range(1, narrow):
                 summaries[place] = order.after(summaries[place])
-            moved[count - 1] = [send(order.after(rows_of(count - 1)), 0, 1)]
+            if waits:
+                moved[count - 1] = [send(order.after(rows_of(count - 1)), 0, 1)]
             galerkin = order.after(galerkin)
             galerkins = [galerkin] + [lax.ppermute(galerkin, "narrow", way) for way in ways]
         else:
             number, hop = step
-            if joined and step == (joined[0], 0):
+            if joined and step == (1, 0):
                 whole = order.after(whole)
-                for part in joined:
-                    low, high = (bound - bounds[joined[0]][0] for bound in bounds[part])
+                for part in range(1, count):
+                    low, high = (bound - bounds[1][0] for bound in bounds[part])
                     moved[part] = [whole[low:high]]
             moving = moved[number][hop] = order.after(moved[number][hop])
             if number == 0 and hop + 1 < hops:

time: 140 us -> 139 us (level)
  starting transfers between devices: 37.7 us -> 42.6 us
  Pallas kernels: 45.8 us -> 42.9 us
  local copies, waits for them, and re-layouts: 15 us -> 13 us
  waiting for transfers between devices: 33.8 us -> 32.3 us
    ppermute x8, starting transfers between devices: 15 us -> 19.3 us  [send(): return lax.ppermute(value, 'narrow', [(owner + source, owner + target)])]
    pallas_call x3, Pallas kernels: 17.5 us -> 15.3 us  [panel(): pl.pallas_call(functools.partial(panel_kernel, pieces=range(pieces), span...]
    cond x46 -> x38, local copies, waits for them, and re-layouts: 9.91 us -> 7.92 us
    ppermute x3, waiting for transfers between devices: 5.54 us -> 3.99 us  [known_owner(): lax.ppermute(galerkin, 'narrow', way)]
  transfers between devices with their start and end apart: 24 -> 24, of which waited for: 9 -> 9; matrix products, arithmetic and copies ran while one was open for 6% -> 6% of each run, Pallas kernels for 26% -> 25%
where the time goes in v1:
time: 139 us; the launch traced here: 136 us
  Pallas kernels  42.9 us (31%)
  starting transfers between devices  42.6 us (31%)
  waiting for transfers between devices  32.3 us (23%)
  local copies, waits for them, and re-layouts  13 us (9%)
  other arithmetic  3.57 us (3%)
    ppermute x8, starting transfers between devices, send(): return lax.ppermute(value, 'narrow', [(owner + source, owner + target)])  19.3 us
    pallas_call x3, Pallas kernels, panel(): pl.pallas_call(functools.partial(panel_kernel, pieces=range(pieces), span...  15.3 us
    ppermute x8, waiting for transfers between devices, send(): return lax.ppermute(value, 'narrow', [(owner + source, owner + target)])  11.4 us
    pallas_call x1, Pallas kernels, interior(): pl.pallas_call(interior_kernel, grid=(subs, comps), in_specs=[SMEM, SMEM,...  10.7 us
    ppermute x4, starting transfers between devices, summed(): lax.ppermute(total, axes, within(group, pairs))  9.35 us
    ppermute x4, waiting for transfers between devices, summed(): lax.ppermute(total, axes, within(group, pairs))  8.18 us
    cond x38, local copies, waits for them, and re-layouts  7.92 us
    pallas_call x1, Pallas kernels, halo_message(): pl.pallas_call(functools.partial(halo_kernel, spans=spans), in_specs=[SME...  5.53 us
  transfers between devices with their start and end apart: 24, of which 9 were waited for; matrix products, arithmetic and copies ran while one was open for 6% of the time, Pallas kernels for 25%

profile of v1, /device:TPU:22, one launch (start us, length us, event | category | flops | bytes accessed | tf_op | source)
XLA Modules:
  0.0 136.2 jit_solution(16449501942329582916)
XLA Ops:
  1.3 134.9 %conditional.1 = (bf16[12288,128]{1,0:T(8,128)(2,1)}, f32[2,96,96]{2,1,0:T(8,128)}) conditional(s32[]{:T(128)} %bitcast.33, (bf16[2,16]{1,0:T(2,128)(2,1)}, s32[2,4,8,128]{3,2,1,0:T(8,128)}, bf16[2,96,3,4,8,128]{5,4,3,2,1,0:T(8,128)(2,1)}, bf16[12288,128]{1,0:T(8,128)(2,1)}, s32[2,96]{1,0:T(2,128)}) %tuple.112, ...), branch_computations={%region_0.1_spmd, %region_1.2_spmd, %region_2.3_spmd} | conditional | flops 69757 | bytes 87678008 | solution.py:819
  2.0 5.5 %halo_message.4 = (bf16[2,290,8,128]{3,2,1,0:T(8,128)(2,1)}, bf16[2,288,8,128]{3,2,1,0:T(8,128)(2,1)S(1)}, bf16[6144,128]{1,0:T(8,128)(2,1)}, bf16[3072,128]{1,0:T(8,128)(2,1)S(1)}) custom-call(f32[2,16]{1,0:T(2,128)S(1)} %convert_element_type.2.table_ref, s32[2,4,8,128]{3,2,1,0:T(8,128)} %get-tuple-element.120.ids_ref, s32[1]{0:T(128)} %bitcast.11.token_ref, ...), custom_call_target="tpu_custom_call" | custom-call | flops 1 | bytes 1 | tf_op jit(solution)/shard_map/cond/branch_1_fun/halo_message/pallas_call | solution.py:94
  7.5 0.9 copy-done.28
  8.4 2.5 %collective-permute-start = (bf16[2,290,8,128]{3,2,1,0:T(8,128)(2,1)}, bf16[2,290,8,128]{3,2,1,0:T(8,128)(2,1)S(1)}, u32[]{:S(2)}, u32[]{:S(2)}) collective-permute-start(bf16[2,290,8,128]{3,2,1,0:T(8,128)(2,1)} %get-tuple-element.150), channel_id=1, source_target_pairs={{1,0},{2,1},{3,2},{9,8},{10,9},{11,10},{17,16},{18,17},{19,18},{25... | collective-permute-start | bytes 3563528 | tf_op jit(solution)/shard_map/cond/branch_1_fun/ppermute | solution.py:671
  11.0 10.7 %interior.4.inner_ref = f32[2,96,96]{2,1,0:T(8,128)S(1)} custom-call(s32[1]{0:T(128)} %bitcast.17.edge_ref, f32[2,16]{1,0:T(2,128)S(1)} %convert_element_type.2.table_ref, s32[2,4,8,128]{3,2,1,0:T(8,128)S(1)} %copy-done.35, bf16[2,96,3,4,8,128]{5,4,3,2,1,0:T(8,128)(2,1)} %get-tuple-element.121.basis_ref, s32[1]{0:T(128)} %bitcast.11.token_ref), custom_call_target="tpu_custom_call" | custom-call | flops 1 | bytes 1 | tf_op jit(solution)/shard_map/cond/branch_1_fun/interior/pallas_call | solution.py:190
  21.7 0.8 slice.20
  23.1 3.6 %collective-permute-done.halo_ref = bf16[2,290,8,128]{3,2,1,0:T(8,128)(2,1)S(1)} collective-permute-done((bf16[2,290,8,128]{3,2,1,0:T(8,128)(2,1)}, bf16[2,290,8,128]{3,2,1,0:T(8,128)(2,1)S(1)}, u32[]{:S(2)}, u32[]{:S(2)}) %collective-permute-start) | collective-permute-done | bytes 1187872 | tf_op jit(solution)/shard_map/cond/branch_1_fun/ppermute | solution.py:671
  26.8 1.0 copy-done
  27.8 0.7 collective-permute-start.5
  28.6 1.7 %collective-permute-start.8 = (bf16[2,290,8,128]{3,2,1,0:T(8,128)(2,1)}, bf16[2,290,8,128]{3,2,1,0:T(8,128)(2,1)}, u32[]{:S(2)}, u32[]{:S(2)}) collective-permute-start(bf16[2,290,8,128]{3,2,1,0:T(8,128)(2,1)} %get-tuple-element.150), channel_id=1, source_target_pairs={{5,4},{6,5},{7,6},{13,12},{14,13},{15,14},{21,20},{22,21},{23,22},... | collective-permute-start | bytes 3563528 | tf_op jit(solution)/shard_map/cond/branch_1_fun/ppermute | solution.py:671
  30.3 1.3 copy-done.1
  31.6 4.5 %face.8 = f32[2,96,96]{2,1,0:T(8,128)S(1)} custom-call(s32[1]{0:T(128)} %bitcast.16.flags_ref, f32[2,16]{1,0:T(2,128)S(1)} %convert_element_type.2.table_ref, s32[2,4,8,128]{3,2,1,0:T(8,128)S(1)} %copy-done.35, bf16[2,288,8,128]{3,2,1,0:T(8,128)(2,1)S(1)} %get-tuple-element.123.last_ref, bf16[2,290,8,128]{3,2,1,0:T(8,128)(2,1)S(1)} %copy-done.1, ...), custom_call_target="tpu_custom_call" | custom-call | flops 1 | bytes 1 | tf_op jit(solution)/shard_map/cond/branch_1_fun/face/pallas_call | solution.py:268
  36.1 1.3 collective-permute-start.2
  37.4 0.8 copy.15.column_ids_ref
  38.2 6.7 %collective-permute-done.2 = f32[2,96,96]{2,1,0:T(8,128)S(1)} collective-permute-done((f32[2,96,96]{2,1,0:T(8,128)S(1)}, f32[2,96,96]{2,1,0:T(8,128)S(1)}, u32[]{:S(2)}, u32[]{:S(2)}) %collective-permute-start.2) | collective-permute-done | bytes 73760 | tf_op jit(solution)/shard_map/cond/branch_1_fun/ppermute | solution.py:694
  44.9 6.7 %collective-permute-start.3 = (f32[2,96,96]{2,1,0:T(8,128)S(1)}, f32[2,96,96]{2,1,0:T(8,128)S(1)}, u32[]{:S(2)}, u32[]{:S(2)}) collective-permute-start(f32[2,96,96]{2,1,0:T(8,128)S(1)} %add.59.rest_0_.refs_2_), channel_id=1, source_target_pairs={{2,1},{10,9},{18,17},{26,25}} | collective-permute-start | bytes 221192 | tf_op jit(solution)/shard_map/cond/branch_1_fun/ppermute | solution.py:694
  51.6 0.7 pad_add_fusion.7.flags_ref
  52.3 1.5 %collective-permute-done.3.rest_1_.refs_3_ = f32[2,96,96]{2,1,0:T(8,128)S(1)} collective-permute-done((f32[2,96,96]{2,1,0:T(8,128)S(1)}, f32[2,96,96]{2,1,0:T(8,128)S(1)}, u32[]{:S(2)}, u32[]{:S(2)}) %collective-permute-start.3) | collective-permute-done | bytes 73760 | tf_op jit(solution)/shard_map/cond/branch_1_fun/ppermute | solution.py:694
  54.4 1.7 %assemble.4 = f32[128,128]{1,0:T(8,128)} custom-call(s32[2]{0:T(128)} %pad_add_fusion.7.flags_ref, s32[1]{0:T(128)} %bitcast.11.token_ref, s32[2,96,1]{2,1,0:T(8,128)} %copy.15.column_ids_ref, s32[2,1,96]{2,1,0:T(1,128)S(1)} %bitcast.38, bf16[12288,128]{1,0:T(8,128)(2,1)} %get-tuple-element.118.slab_ref, bf16[128,128]{1,0:T(8,128)(2,1)} %copy-done.64, ...), custom_call_target="tpu_custom_call" | custom-call | flops 1 | bytes 1 | tf_op jit(solution)/shard_map/cond/branch_1_fun/assemble/pallas_call | solution.py:325
  56.1 1.3 collective-permute-start.4
  58.1 1.9 %slice.21 = bf16[2048,128]{1,0:T(8,128)(2,1)} slice(bf16[12288,128]{1,0:T(8,128)(2,1)} %get-tuple-element.118.slab_ref), slice={[9216:11264], [0:128]} | slice | bytes 1048576 | tf_op jit(solution)/shard_map/cond/branch_1_fun/slice | solution.py:653
  59.9 0.9 add.60
  60.8 1.3 collective-permute-start.7
  63.4 3.6 %collective-permute-done.7 = f32[128,128]{1,0:T(8,128)S(1)} collective-permute-done((f32[128,128]{1,0:T(8,128)S(1)}, f32[128,128]{1,0:T(8,128)S(1)}, u32[]{:S(2)}, u32[]{:S(2)}) %collective-permute-start.7) | collective-permute-done | bytes 65568 | tf_op jit(solution)/shard_map/cond/branch_1_fun/ppermute | solution.py:747
  67.0 1.3 collective-permute-start.9
  68.3 0.9 collective-permute-done.9.refs_1_
  69.2 1.3 collective-permute-start.21
  70.4 1.3 collective-permute-start.15
  71.7 8.4 %collective-permute-done.4.rest_0_ = bf16[3072,128]{1,0:T(8,128)(2,1)} collective-permute-done((bf16[3072,128]{1,0:T(8,128)(2,1)}, bf16[3072,128]{1,0:T(8,128)(2,1)}, u32[]{:S(2)}, u32[]{:S(2)}) %collective-permute-start.4) | collective-permute-done | bytes 786464 | tf_op jit(solution)/shard_map/cond/branch_1_fun/ppermute | solution.py:656
  80.1 1.3 collective-permute-start.20
  83.4 1.9 %factorize.4 = (bf16[384,128]{1,0:T(8,128)(2,1)}, f32[128,128]{1,0:T(8,128)}, f32[2,96,96]{2,1,0:T(8,128)}) custom-call(s32[2]{0:T(128)} %pad_add_fusion.6.flags_ref, s32[1]{0:T(128)} %bitcast.11.token_ref, f32[128,128]{1,0:T(8,128)} %copy-done.47, f32[128,128]{1,0:T(8,128)} %copy-done.61, f32[2,96,96]{2,1,0:T(8,128)} %copy-done.37, ...), custom_call_target="tpu_custom_call" | custom-call | flops 1 | bytes 1 | tf_op jit(solution)/shard_map/cond/branch_1_fun/factorize/pallas_call | solution.py:397
  85.3 1.3 collective-permute-start.14
  87.2 3.0 %collective-permute-done.15.rest_0_ = bf16[2048,128]{1,0:T(8,128)(2,1)S(1)} collective-permute-done((bf16[2048,128]{1,0:T(8,128)(2,1)}, bf16[2048,128]{1,0:T(8,128)(2,1)S(1)}, u32[]{:S(2)}, u32[]{:S(2)}) %collective-permute-start.15) | collective-permute-done | bytes 524320 | tf_op jit(solution)/shard_map/cond/branch_1_fun/ppermute | solution.py:656
  90.9 1.7 %slice.19 = bf16[1024,128]{1,0:T(8,128)(2,1)} slice(bf16[12288,128]{1,0:T(8,128)(2,1)} %get-tuple-element.118.slab_ref), slice={[11264:12288], [0:128]} | slice | bytes 524288 | tf_op jit(solution)/shard_map/cond/branch_1_fun/slice | solution.py:653
  93.2 2.1 %collective-permute-start.22 = (bf16[2048,128]{1,0:T(8,128)(2,1)S(1)}, bf16[2048,128]{1,0:T(8,128)(2,1)}, u32[]{:S(2)}, u32[]{:S(2)}) collective-permute-start(bf16[2048,128]{1,0:T(8,128)(2,1)S(1)} %collective-permute-done.15.rest_0_), channel_id=1, source_target_pairs={{2,3},{6,7},{10,11},{14,15},{18,19},{22,23},{26,27},{30,31}} | collective-permute-start | bytes 1572872 | tf_op jit(solution)/shard_map/cond/branch_1_fun/ppermute | solution.py:656
  95.2 1.3 collective-permute-start.19
  96.5 1.3 collective-permute-start.16
  98.4 4.0 %collective-permute-done.19.rest_1_ = f32[2,96,96]{2,1,0:T(8,128)S(1)} collective-permute-done((f32[2,96,96]{2,1,0:T(8,128)}, f32[2,96,96]{2,1,0:T(8,128)S(1)}, u32[]{:S(2)}, u32[]{:S(2)}) %collective-permute-start.19) | collective-permute-done | bytes 73760 | tf_op jit(solution)/shard_map/cond/branch_1_fun/ppermute | solution.py:765
  103.2 1.3 collective-permute-start.17
  104.5 1.8 %added.4 = (f32[128,128]{1,0:T(8,128)}, f32[2,96,96]{2,1,0:T(8,128)}) custom-call(s32[3]{0:T(128)} %pad_add_fusion.8.flags_ref, s32[1]{0:T(128)} %bitcast.11.token_ref, s32[2,96,1]{2,1,0:T(8,128)} %copy.15.column_ids_ref, s32[2,1,96]{2,1,0:T(1,128)S(1)} %bitcast.39, f32[2,96,96]{2,1,0:T(8,128)} %get-tuple-element.175.rest_0_, f32[2,96,96]{2,1,0:T(8,128)} %copy-done.54, ...), custom_call_target="tpu_custom_call" | custom-call | flops 1 | bytes 1 | tf_op jit(solution)/shard_map/cond/branch_1_fun/added/pallas_call | solution.py:475
  106.3 0.8 copy-done.6
  107.2 0.9 copy-done.10
  108.1 1.0 prepare.4
  109.1 4.8 %panel.11 = (bf16[12288,128]{1,0:T(8,128)(2,1)S(1)}, s32[1]{0:T(128)}) custom-call(s32[4]{0:T(128)S(1)} %pad_add_fusion.5.flags_ref, s32[1]{0:T(128)} %bitcast.11.token_ref, bf16[128,128]{1,0:T(8,128)(2,1)S(1)} %get-tuple-element.189.lower_ref, bf16[512,256]{1,0:T(8,128)(2,1)S(1)} %get-tuple-element.190.weights_ref, ...), custom_call_target="tpu_custom_call" | custom-call | flops 1 | bytes 1 | tf_op jit(solution)/shard_map/cond/branch_1_fun/panel/pallas_call | solution.py:583
  113.9 10.0 %collective-permute-start.23 = (bf16[1024,128]{1,0:T(8,128)(2,1)S(1)}, bf16[1024,128]{1,0:T(8,128)(2,1)S(1)}, u32[]{:S(2)}, u32[]{:S(2)}) collective-permute-start(bf16[1024,128]{1,0:T(8,128)(2,1)S(1)} %collective-permute-done.16.rest_2_), channel_id=1, source_target_pairs={{2,3},{6,7},{10,11},{14,15},{18,19},{22,23},{26,27},{30,31}} | collective-permute-start | bytes 786440 | tf_op jit(solution)/shard_map/cond/branch_1_fun/ppermute | solution.py:656
  123.9 6.9 %panel.12 = (bf16[12288,128]{1,0:T(8,128)(2,1)S(1)}, s32[1]{0:T(128)}) custom-call(s32[4]{0:T(128)S(1)} %pad_add_fusion.5.flags_ref, s32[1]{0:T(128)} %get-tuple-element.194.token_ref, bf16[128,128]{1,0:T(8,128)(2,1)S(1)} %get-tuple-element.189.lower_ref, bf16[512,256]{1,0:T(8,128)(2,1)S(1)} %get-tuple-element.190.weights_ref, ...), custom_call_target="tpu_custom_call", output_to_operand_aliasing={{0}: (9, {})} | custom-call | flops 1 | bytes 1 | tf_op jit(solution)/shard_map/cond/branch_1_fun/panel/pallas_call | solution.py:583
  130.9 3.6 %panel.13 = (bf16[12288,128]{1,0:T(8,128)(2,1)S(1)}, s32[1]{0:T(128)}) custom-call(s32[4]{0:T(128)S(1)} %pad_add_fusion.5.flags_ref, s32[1]{0:T(128)} %get-tuple-element.198.token_ref, bf16[128,128]{1,0:T(8,128)(2,1)S(1)} %get-tuple-element.189.lower_ref, bf16[512,256]{1,0:T(8,128)(2,1)S(1)} %get-tuple-element.190.weights_ref, ...), custom_call_target="tpu_custom_call", output_to_operand_aliasing={{0}: (11, {})} | custom-call | flops 1 | bytes 1 | tf_op jit(solution)/shard_map/cond/branch_1_fun/panel/pallas_call | solution.py:583
  134.5 1.7 %copy-done.32 = bf16[12288,128]{1,0:T(8,128)(2,1)} copy-done((bf16[12288,128]{1,0:T(8,128)(2,1)}, bf16[12288,128]{1,0:T(8,128)(2,1)S(1)}, u32[]{:S(2)}) %copy-start.32) | copy-done | bytes 3145752 | tf_op jit(solution)/shard_map/cond
  (64 shorter events, 9.2 us)
Async XLA Ops:
  2.0 9.0 %copy-start.35 = (s32[2,4,8,128]{3,2,1,0:T(8,128)S(1)}, s32[2,4,8,128]{3,2,1,0:T(8,128)}, u32[]{:S(2)}) copy-start(s32[2,4,8,128]{3,2,1,0:T(8,128)} %get-tuple-element.120.ids_ref) | copy-start | bytes 98308 | tf_op jit(solution)/shard_map/cond
  7.5 0.9 copy-start.28
  8.4 18.4 %collective-permute-start = (bf16[2,290,8,128]{3,2,1,0:T(8,128)(2,1)}, bf16[2,290,8,128]{3,2,1,0:T(8,128)(2,1)S(1)}, u32[]{:S(2)}, u32[]{:S(2)}) collective-permute-start(bf16[2,290,8,128]{3,2,1,0:T(8,128)(2,1)} %get-tuple-element.150), channel_id=1, source_target_pairs={{1,0},{2,1},{3,2},{9,8},{10,9},{11,10},{17,16},{18,17},{19,18},{25... | collective-permute-start | bytes 3563528 | tf_op jit(solution)/shard_map/cond/branch_1_fun/ppermute | solution.py:671
  21.7 15.7 %copy-start.59 = (s32[2,96]{1,0:T(2,128)S(1)}, s32[2,96]{1,0:T(2,128)}, u32[]{:S(2)}) copy-start(s32[2,96]{1,0:T(2,128)} %get-tuple-element.140) | copy-start | bytes 2308 | tf_op jit(solution)/shard_map/cond
  22.5 0.7 collective-permute-start.1
  23.1 30.6 %copy-start.64 = (bf16[128,128]{1,0:T(8,128)(2,1)}, bf16[128,128]{1,0:T(8,128)(2,1)S(1)}, u32[]{:S(2)}) copy-start(bf16[128,128]{1,0:T(8,128)(2,1)S(1)} %collective-permute-done.1.head_ref) | copy-start | bytes 98308 | tf_op jit(solution)/shard_map/cond
  26.8 1.0 copy-start
  27.8 41.3 %collective-permute-start.5 = (bf16[6144,128]{1,0:T(8,128)(2,1)}, bf16[6144,128]{1,0:T(8,128)(2,1)S(1)}, u32[]{:S(2)}, u32[]{:S(2)}) collective-permute-start(bf16[6144,128]{1,0:T(8,128)(2,1)} %get-tuple-element.145), channel_id=1, source_target_pairs={{1,3},{5,7},{9,11},{13,15},{17,19},{21,23},{25,27},{29,31}} | collective-permute-start | bytes 4718600 | tf_op jit(solution)/shard_map/cond/branch_1_fun/ppermute | solution.py:656
  28.6 33.5 %collective-permute-start.8 = (bf16[2,290,8,128]{3,2,1,0:T(8,128)(2,1)}, bf16[2,290,8,128]{3,2,1,0:T(8,128)(2,1)}, u32[]{:S(2)}, u32[]{:S(2)}) collective-permute-start(bf16[2,290,8,128]{3,2,1,0:T(8,128)(2,1)} %get-tuple-element.150), channel_id=1, source_target_pairs={{5,4},{6,5},{7,6},{13,12},{14,13},{15,14},{21,20},{22,21},{23,22},... | collective-permute-start | bytes 3563528 | tf_op jit(solution)/shard_map/cond/branch_1_fun/ppermute | solution.py:671
  30.3 1.3 copy-start.1
  36.1 8.8 %collective-permute-start.2 = (f32[2,96,96]{2,1,0:T(8,128)S(1)}, f32[2,96,96]{2,1,0:T(8,128)S(1)}, u32[]{:S(2)}, u32[]{:S(2)}) collective-permute-start(f32[2,96,96]{2,1,0:T(8,128)S(1)} %face.8), channel_id=1, source_target_pairs={{0,1},{3,2},{8,9},{11,10},{16,17},{19,18},{24,25},{27,26}} | collective-permute-start | bytes 221192 | tf_op jit(solution)/shard_map/cond/branch_1_fun/ppermute | solution.py:694
  44.8 8.9 %copy-start.37 = (f32[2,96,96]{2,1,0:T(8,128)}, f32[2,96,96]{2,1,0:T(8,128)S(1)}, u32[]{:S(2)}) copy-start(f32[2,96,96]{2,1,0:T(8,128)S(1)} %add.59.rest_0_.refs_2_) | copy-start | bytes 221188 | tf_op jit(solution)/shard_map/cond
  44.9 8.9 %collective-permute-start.3 = (f32[2,96,96]{2,1,0:T(8,128)S(1)}, f32[2,96,96]{2,1,0:T(8,128)S(1)}, u32[]{:S(2)}, u32[]{:S(2)}) collective-permute-start(f32[2,96,96]{2,1,0:T(8,128)S(1)} %add.59.rest_0_.refs_2_), channel_id=1, source_target_pairs={{2,1},{10,9},{18,17},{26,25}} | collective-permute-start | bytes 221192 | tf_op jit(solution)/shard_map/cond/branch_1_fun/ppermute | solution.py:694
  53.8 0.7 copy-start.40
  56.1 24.0 %collective-permute-start.4 = (bf16[3072,128]{1,0:T(8,128)(2,1)}, bf16[3072,128]{1,0:T(8,128)(2,1)}, u32[]{:S(2)}, u32[]{:S(2)}) collective-permute-start(bf16[3072,128]{1,0:T(8,128)(2,1)} %copy-done.28), channel_id=1, source_target_pairs={{1,2},{5,6},{9,10},{13,14},{17,18},{21,22},{25,26},{29,30}} | collective-permute-start | bytes 2359304 | tf_op jit(solution)/shard_map/cond/branch_1_fun/ppermute | solution.py:656
  57.4 2.6 %collective-permute-start.6 = (f32[128,128]{1,0:T(8,128)}, f32[128,128]{1,0:T(8,128)S(1)}, u32[]{:S(2)}, u32[]{:S(2)}) collective-permute-start(f32[128,128]{1,0:T(8,128)} %assemble.4), channel_id=1, source_target_pairs={{0,16},{9,25},{18,2},{27,11}} | collective-permute-start | bytes 196616 | tf_op jit(solution)/shard_map/cond/branch_1_fun/ppermute | solution.py:747
  60.8 6.2 %collective-permute-start.7 = (f32[128,128]{1,0:T(8,128)S(1)}, f32[128,128]{1,0:T(8,128)S(1)}, u32[]{:S(2)}, u32[]{:S(2)}) collective-permute-start(f32[128,128]{1,0:T(8,128)S(1)} %add.60), channel_id=1, source_target_pairs={{0,8},{16,24},{9,1},{25,17},{18,26},{2,10},{27,19},{11,3}} | collective-permute-start | bytes 196616 | tf_op jit(solution)/shard_map/cond/branch_1_fun/ppermute | solution.py:747
  62.7 5.6 %collective-permute-start.10 = (f32[2,96,96]{2,1,0:T(8,128)S(1)}, f32[2,96,96]{2,1,0:T(8,128)S(1)}, u32[]{:S(2)}, u32[]{:S(2)}) collective-permute-start(f32[2,96,96]{2,1,0:T(8,128)S(1)} %face.9), channel_id=1, source_target_pairs={{4,5},{7,6},{12,13},{15,14},{20,21},{23,22},{28,29},{31,30}} | collective-permute-start | bytes 221192 | tf_op jit(solution)/shard_map/cond/branch_1_fun/ppermute | solution.py:694
  67.0 15.8 %copy-start.47 = (f32[128,128]{1,0:T(8,128)}, f32[128,128]{1,0:T(8,128)S(1)}, u32[]{:S(2)}) copy-start(f32[128,128]{1,0:T(8,128)S(1)} %add.61.refs_0_) | copy-start | bytes 196612 | tf_op jit(solution)/shard_map/cond
  67.0 2.2 %collective-permute-start.9 = (f32[128,128]{1,0:T(8,128)S(1)}, f32[128,128]{1,0:T(8,128)S(1)}, u32[]{:S(2)}, u32[]{:S(2)}) collective-permute-start(f32[128,128]{1,0:T(8,128)S(1)} %add.61.refs_0_), channel_id=1, source_target_pairs={{0,4},{8,12},{16,20},{24,28},{9,13},{1,5},{25,29},{17,21},{18,22},... | collective-permute-start | bytes 196616 | tf_op jit(solution)/shard_map/cond/branch_1_fun/ppermute | solution.py:747
  69.1 13.6 %copy-start.61 = (f32[128,128]{1,0:T(8,128)}, f32[128,128]{1,0:T(8,128)S(1)}, u32[]{:S(2)}) copy-start(f32[128,128]{1,0:T(8,128)S(1)} %collective-permute-done.9.refs_1_) | copy-start | bytes 196612 | tf_op jit(solution)/shard_map/cond
  69.2 54.7 %collective-permute-start.21 = (bf16[6144,128]{1,0:T(8,128)(2,1)S(1)}, bf16[6144,128]{1,0:T(8,128)(2,1)}, u32[]{:S(2)}, u32[]{:S(2)}) collective-permute-start(bf16[6144,128]{1,0:T(8,128)(2,1)S(1)} %collective-permute-done.5.rest_1_), channel_id=1, source_target_pairs={{3,2},{7,6},{11,10},{15,14},{19,18},{23,22},{27,26},{31,30}} | collective-permute-start | bytes 4718600 | tf_op jit(solution)/shard_map/cond/branch_1_fun/ppermute | solution.py:656
  70.4 19.8 %collective-permute-start.15 = (bf16[2048,128]{1,0:T(8,128)(2,1)}, bf16[2048,128]{1,0:T(8,128)(2,1)S(1)}, u32[]{:S(2)}, u32[]{:S(2)}) collective-permute-start(bf16[2048,128]{1,0:T(8,128)(2,1)} %slice.21), channel_id=1, source_target_pairs={{1,2},{5,6},{9,10},{13,14},{17,18},{21,22},{25,26},{29,30}} | collective-permute-start | bytes 1572872 | tf_op jit(solution)/shard_map/cond/branch_1_fun/ppermute | solution.py:656
  80.1 29.0 %collective-permute-start.20 = (bf16[3072,128]{1,0:T(8,128)(2,1)}, bf16[3072,128]{1,0:T(8,128)(2,1)S(1)}, u32[]{:S(2)}, u32[]{:S(2)}) collective-permute-start(bf16[3072,128]{1,0:T(8,128)(2,1)} %collective-permute-done.4.rest_0_), channel_id=1, source_target_pairs={{2,3},{6,7},{10,11},{14,15},{18,19},{22,23},{26,27},{30,31}} | collective-permute-start | bytes 2359304 | tf_op jit(solution)/shard_map/cond/branch_1_fun/ppermute | solution.py:656
  81.5 1.3 copy-start.45
  81.5 1.3 collective-permute-start.11
  82.8 0.6 copy-start.52
  85.3 7.9 %collective-permute-start.14 = (bf16[384,128]{1,0:T(8,128)(2,1)}, bf16[384,128]{1,0:T(8,128)(2,1)S(1)}, u32[]{:S(2)}, u32[]{:S(2)}) collective-permute-start(bf16[384,128]{1,0:T(8,128)(2,1)} %get-tuple-element.165.rest_0_), channel_id=1, source_target_pairs={{1,2},{5,6},{9,10},{13,14},{17,18},{21,22},{25,26},{29,30}} | collective-permute-start | bytes 294920 | tf_op jit(solution)/shard_map/cond/branch_1_fun/ppermute | solution.py:758
  86.6 8.7 %collective-permute-start.13 = (bf16[384,128]{1,0:T(8,128)(2,1)}, bf16[384,128]{1,0:T(8,128)(2,1)S(1)}, u32[]{:S(2)}, u32[]{:S(2)}) collective-permute-start(bf16[384,128]{1,0:T(8,128)(2,1)} %get-tuple-element.165.rest_0_), channel_id=1, source_target_pairs={{1,3},{5,7},{9,11},{13,15},{17,19},{21,23},{25,27},{29,31}} | collective-permute-start | bytes 294920 | tf_op jit(solution)/shard_map/cond/branch_1_fun/ppermute | solution.py:758
  90.3 5.0 %collective-permute-start.12 = (bf16[384,128]{1,0:T(8,128)(2,1)}, bf16[384,128]{1,0:T(8,128)(2,1)S(1)}, u32[]{:S(2)}, u32[]{:S(2)}) collective-permute-start(bf16[384,128]{1,0:T(8,128)(2,1)} %get-tuple-element.165.rest_0_), channel_id=1, source_target_pairs={{1,0},{5,4},{9,8},{13,12},{17,16},{21,20},{25,24},{29,28}} | collective-permute-start | bytes 294920 | tf_op jit(solution)/shard_map/cond/branch_1_fun/ppermute | solution.py:758
  93.2 37.7 %collective-permute-start.22 = (bf16[2048,128]{1,0:T(8,128)(2,1)S(1)}, bf16[2048,128]{1,0:T(8,128)(2,1)}, u32[]{:S(2)}, u32[]{:S(2)}) collective-permute-start(bf16[2048,128]{1,0:T(8,128)(2,1)S(1)} %collective-permute-done.15.rest_0_), channel_id=1, source_target_pairs={{2,3},{6,7},{10,11},{14,15},{18,19},{22,23},{26,27},{30,31}} | collective-permute-start | bytes 1572872 | tf_op jit(solution)/shard_map/cond/branch_1_fun/ppermute | solution.py:656
  95.2 7.2 %collective-permute-start.19 = (f32[2,96,96]{2,1,0:T(8,128)}, f32[2,96,96]{2,1,0:T(8,128)S(1)}, u32[]{:S(2)}, u32[]{:S(2)}) collective-permute-start(f32[2,96,96]{2,1,0:T(8,128)} %get-tuple-element.175.rest_0_), channel_id=1, source_target_pairs={{1,2},{5,6},{9,10},{13,14},{17,18},{21,22},{25,26},{29,30}} | collective-permute-start | bytes 221192 | tf_op jit(solution)/shard_map/cond/branch_1_fun/ppermute | solution.py:765
  96.5 17.4 %collective-permute-start.16 = (bf16[1024,128]{1,0:T(8,128)(2,1)}, bf16[1024,128]{1,0:T(8,128)(2,1)S(1)}, u32[]{:S(2)}, u32[]{:S(2)}) collective-permute-start(bf16[1024,128]{1,0:T(8,128)(2,1)} %slice.19), channel_id=1, source_target_pairs={{1,2},{5,6},{9,10},{13,14},{17,18},{21,22},{25,26},{29,30}} | collective-permute-start | bytes 786440 | tf_op jit(solution)/shard_map/cond/branch_1_fun/ppermute | solution.py:656
  102.4 2.1 %copy-start.54 = (f32[2,96,96]{2,1,0:T(8,128)}, f32[2,96,96]{2,1,0:T(8,128)S(1)}, u32[]{:S(2)}) copy-start(f32[2,96,96]{2,1,0:T(8,128)S(1)} %collective-permute-done.19.rest_1_) | copy-start | bytes 221188 | tf_op jit(solution)/shard_map/cond
  102.4 0.7 collective-permute-start.18
  103.1 1.3 copy-start.57
  103.2 1.4 %collective-permute-start.17 = (f32[2,96,96]{2,1,0:T(8,128)}, f32[2,96,96]{2,1,0:T(8,128)}, u32[]{:S(2)}, u32[]{:S(2)}) collective-permute-start(f32[2,96,96]{2,1,0:T(8,128)} %get-tuple-element.175.rest_0_), channel_id=1, source_target_pairs={{1,0},{5,4},{9,8},{13,12},{17,16},{21,20},{25,24},{29,28}} | collective-permute-start | bytes 221192 | tf_op jit(solution)/shard_map/cond/branch_1_fun/ppermute | solution.py:765
  106.3 0.8 copy-start.6
  107.2 0.9 copy-start.10
  109.1 14.8 %copy-start.22 = (f32[128,128]{1,0:T(8,128)S(1)}, f32[128,128]{1,0:T(8,128)}, u32[]{:S(2)}) copy-start(f32[128,128]{1,0:T(8,128)} %get-tuple-element.195.added_ref) | copy-start | bytes 196612 | tf_op jit(solution)/shard_map/cond
  109.1 14.8 %copy-start.30 = (bf16[12288,128]{1,0:T(8,128)(2,1)S(1)}, bf16[12288,128]{1,0:T(8,128)(2,1)}, u32[]{:S(2)}) copy-start(bf16[12288,128]{1,0:T(8,128)(2,1)} %get-tuple-element.118.slab_ref) | copy-start | bytes 9437188 | tf_op jit(solution)/shard_map/cond
  113.9 16.9 %collective-permute-start.23 = (bf16[1024,128]{1,0:T(8,128)(2,1)S(1)}, bf16[1024,128]{1,0:T(8,128)(2,1)S(1)}, u32[]{:S(2)}, u32[]{:S(2)}) collective-permute-start(bf16[1024,128]{1,0:T(8,128)(2,1)S(1)} %collective-permute-done.16.rest_2_), channel_id=1, source_target_pairs={{2,3},{6,7},{10,11},{14,15},{18,19},{22,23},{26,27},{30,31}} | collective-permute-start | bytes 786440 | tf_op jit(solution)/shard_map/cond/branch_1_fun/ppermute | solution.py:656
  134.5 1.7 %copy-start.32 = (bf16[12288,128]{1,0:T(8,128)(2,1)}, bf16[12288,128]{1,0:T(8,128)(2,1)S(1)}, u32[]{:S(2)}) copy-start(bf16[12288,128]{1,0:T(8,128)(2,1)S(1)} %get-tuple-element.286) | copy-start | bytes 9437188 | tf_op jit(solution)/shard_map/cond

commit v2 on v1

--- a/solution.py
+++ b/solution.py
@@ -15,12 +15,12 @@
 SMEM = pl.BlockSpec(memory_space=pltpu.SMEM)
 PLANS = {
     1: (
-        (12, 6, 6),
+        (12, 8, 4),
         False,
         True,
         (
             "assemble", "next", "spread", "others", "spread", "more", "spread", (0, 0), "factor", "summary",
-            "sums", ("panel", 0, 2), ("panel", 2, 3),
+            "added", ("panel", 0, 2), "sums", ("panel", 2, 3),
         ),
     ),
     2: (
@@ -29,7 +29,7 @@
         True,
         (
             "assemble", "next", "spread", "others", "spread", "more", "spread", (0, 0), (1, 0), "factor", (2, 0),
-            "summary", "sums", ("panel", 1, 2), (3, 0), ("panel", 0, 1), ("panel", 2, 4),
+            "summary", "added", ("panel", 1, 2), (3, 0), ("panel", 0, 1), "sums", ("panel", 2, 4),
         ),
     ),
     3: (
@@ -38,7 +38,7 @@
         False,
         (
             "assemble", "next", "spread", "others", "spread", "more", "spread", (0, 0), "factor", (1, 0), "summary",
-            (0, 1), (1, 1), (2, 0), ("panel", 1, 2), (2, 1), "sums", ("panel", 0, 1), ("panel", 2, 3),
+            (0, 1), (1, 1), (2, 0), ("panel", 1, 2), (2, 1), "added", ("panel", 0, 1), "sums", ("panel", 2, 3),
         ),
     ),
 }
@@ -458,28 +458,21 @@
     )(flags, token, head, *summaries)
 
 
-def added_kernel(flags_ref, token_ref, column_ids_ref, row_ids_ref, *rest, sources):
-    sum_refs, (added_ref, gal_ref) = rest[:sources], rest[sources:]
-    for number, sum_ref in enumerate(sum_refs):
-
-        @pl.when(flags_ref[0] == number)
-        def _(sum_ref=sum_ref):
-            gal_ref[...] = sum_ref[...]
-
-    @pl.when((flags_ref[1] == 2) & (flags_ref[2] == 1))
-    def _():
-        added_ref[...] = spread(gal_ref, column_ids_ref, row_ids_ref, added_ref.shape[0])
-
-
-def added_of(flags, token, ids, sums, size):
+def added_kernel(flags_ref, token_ref, column_ids_ref, row_ids_ref, sum_ref, added_ref):
+    @pl.when(flags_ref[0] == 1)
+    def _():
+        added_ref[...] = spread(sum_ref, column_ids_ref, row_ids_ref, added_ref.shape[0])
+
+
+def added_of(flags, token, ids, galerkin, size):
     return pl.pallas_call(
-        functools.partial(added_kernel, sources=len(sums)),
-        in_specs=[SMEM, ANY] + [VMEM] * (2 + len(sums)),
-        out_specs=[VMEM] * 2,
-        out_shape=[jax.ShapeDtypeStruct((size, size), F32), jax.ShapeDtypeStruct(sums[0].shape, F32)],
+        added_kernel,
+        in_specs=[SMEM, ANY, VMEM, VMEM, VMEM],
+        out_specs=VMEM,
+        out_shape=jax.ShapeDtypeStruct((size, size), F32),
         cost_estimate=LIGHT,
         name="added",
-    )(flags, token, ids[:, :, None], ids[:, None, :], *sums)
+    )(flags, token, ids[:, :, None], ids[:, None, :], galerkin)
 
 
 def panel_kernel(
@@ -657,7 +650,7 @@
 
     order = Order(settings(mode))
 
-    ways = [((n * stride) * narrow + owner, (n * stride) * narrow + n) for n in range(owner + 1, narrow)]
+    holders = [((n * stride) * narrow + owner, (n * stride) * narrow + n) for n in range(owner + 1, narrow)]
     moved = {}
 
     groups = [[w for w in range(wide) if w % stride == 0], [w for w in range(wide) if w % stride]]
@@ -676,7 +669,7 @@
     halos = [halo_of(groups[0], first)]
     edge = (narrow_index == 0).astype(jnp.int32).reshape(1)
     inner = order.after(interior(edge, table, material_ids, coarse_basis, order.token))
-    head = order.after(lax.ppermute(order.after(coarse_slab[:block]), axes, ways))
+    head = order.after(lax.ppermute(order.after(coarse_slab[:block]), axes, holders))
     halos[0] = order.after(halos[0])
     moved[0] = [send(order.after(begun[0]), 0, hops)]
     for group in groups[1:]:
@@ -715,11 +708,14 @@
             result, order.token = panel(
                 flags, order.token, lower, weights, rows, added if begin == 0 else head, coarse_slab, parts, result, bounds[begin][0], 2 * unit
             )
+        elif step == "added":
+            added = added_of(settings(mode), order.token, coarse_ids, galerkin, block)
+            added = order.after(lax.ppermute(added, axes, holders))
+            if waits:
+                moved[count - 1] = [send(order.after(rows_of(count - 1)), 0, 1)]
         elif step == "sums":
-            for place in range(1, narrow):
-                galerkins[place] = order.after(galerkins[place])
-            added, galerkin = added_of(settings(choice, mode, own), order.token, coarse_ids, galerkins, block)
-            added = order.after(added)
+            galerkins = [order.after(part) for part in galerkins]
+            galerkin = jnp.where(narrow_index == owner, galerkin, sum(galerkins))
         elif step == "next":
             if joined:
                 whole = send(order.after(begun[1]), 0, 1)
@@ -759,10 +755,8 @@
         elif step == "summary":
             for place in range(1, narrow):
                 summaries[place] = order.after(summaries[place])
-            if waits:
-                moved[count - 1] = [send(order.after(rows_of(count - 1)), 0, 1)]
             galerkin = order.after(galerkin)
-            galerkins = [galerkin] + [lax.ppermute(galerkin, "narrow", way) for way in ways]
+            galerkins = [lax.ppermute(galerkin, "narrow", way) for way in ways]
         else:
             number, hop = step
             if joined and step == (1, 0):
@@ -802,7 +796,7 @@
     summary, _, galerkin = factorize(settings(1, 0), first, [diagonal], [parts])
     head = broadcast(message, "wide", narrow_index * stride)
     weights, rows, lower = prepare(settings(0, mode), settings(mode), head, [summary])
-    added, galerkin = added_of(settings(0, mode, own), weights, coarse_ids, [galerkin], head.shape[0])
+    added = added_of(settings(1), weights, coarse_ids, galerkin, head.shape[0])
     flags = settings(mode, kind, own, which)
     tile = coarse_slab.shape[0] // 12
     result, _ = panel(flags, flags, lower, weights, rows, added, coarse_slab, [[column]], None, 0, tile)

time: 139 us -> 168 us (1.21)
  the two profiles are of different devices: /device:TPU:22 before, /device:TPU:20 now
where the time goes in v2:
time: 168 us; the launch traced here: 167 us
  waiting for transfers between devices  57.4 us (34%)
  Pallas kernels  46.8 us (28%)
  starting transfers between devices  41.7 us (25%)
  local copies, waits for them, and re-layouts  14.9 us (9%)
  other arithmetic  3.54 us (2%)
    ppermute x3, waiting for transfers between devices, known_owner(): lax.ppermute(summary, 'narrow', way)  27.2 us
    pallas_call x3, Pallas kernels, panel(): pl.pallas_call(functools.partial(panel_kernel, pieces=range(pieces), span...  18.4 us
    ppermute x8, starting transfers between devices, send(): return lax.ppermute(value, 'narrow', [(owner + source, owner + target)])  15.9 us
    cond x52, local copies, waits for them, and re-layouts  11.8 us
    pallas_call x1, Pallas kernels, interior(): pl.pallas_call(interior_kernel, grid=(subs, comps), in_specs=[SMEM, SMEM,...  10.7 us
    ppermute x8, waiting for transfers between devices, send(): return lax.ppermute(value, 'narrow', [(owner + source, owner + target)])  9.85 us
    ppermute x3, starting transfers between devices, known_owner(): lax.ppermute(message, axes, holder_pairs(wide, narrow, distance))  8.63 us
    ppermute x4, waiting for transfers between devices, summed(): lax.ppermute(total, axes, within(group, pairs))  7.14 us
  transfers between devices with their start and end apart: 25, of which 10 were waited for; matrix products, arithmetic and copies ran while one was open for 4% of the time, Pallas kernels for 22%

profile of v2, /device:TPU:20, one launch (start us, length us, event | category | flops | bytes accessed | tf_op | source)
XLA Modules:
  0.0 166.7 jit_solution(12234245700574582709)
XLA Ops:
  1.3 165.2 %conditional.1 = (bf16[12288,128]{1,0:T(8,128)(2,1)}, f32[2,96,96]{2,1,0:T(8,128)}) conditional(s32[]{:T(128)} %bitcast.33, (bf16[2,16]{1,0:T(2,128)(2,1)}, s32[2,4,8,128]{3,2,1,0:T(8,128)}, bf16[2,96,3,4,8,128]{5,4,3,2,1,0:T(8,128)(2,1)}, bf16[12288,128]{1,0:T(8,128)(2,1)}, s32[2,96]{1,0:T(2,128)}) %tuple.112, ...), branch_computations={%region_0.1_spmd, %region_1.2_spmd, %region_2.3_spmd} | conditional | flops 125047 | bytes 90668048 | solution.py:813
  2.0 5.8 %halo_message.3 = (bf16[2,290,8,128]{3,2,1,0:T(8,128)(2,1)}, bf16[2,288,8,128]{3,2,1,0:T(8,128)(2,1)S(1)}, bf16[6144,128]{1,0:T(8,128)(2,1)}, bf16[6144,128]{1,0:T(8,128)(2,1)S(1)}) custom-call(f32[2,16]{1,0:T(2,128)S(1)} %convert_element_type.0.table_ref, s32[2,4,8,128]{3,2,1,0:T(8,128)} %get-tuple-element.31.ids_ref, s32[1]{0:T(128)} %bitcast.token_ref.flags_ref, ...), custom_call_target="tpu_custom_call" | custom-call | flops 1 | bytes 1 | tf_op jit(solution)/shard_map/cond/branch_0_fun/halo_message/pallas_call | solution.py:94
  7.8 1.2 copy-done.22
  8.9 2.3 %collective-permute-start.45 = (bf16[2,290,8,128]{3,2,1,0:T(8,128)(2,1)}, bf16[2,290,8,128]{3,2,1,0:T(8,128)(2,1)S(1)}, u32[]{:S(2)}, u32[]{:S(2)}) collective-permute-start(bf16[2,290,8,128]{3,2,1,0:T(8,128)(2,1)} %get-tuple-element.60), channel_id=1, source_target_pairs={{1,0},{2,1},{3,2},{9,8},{10,9},{11,10},{17,16},{18,17},{19,18},{25... | collective-permute-start | bytes 3563528 | tf_op jit(solution)/shard_map/cond/branch_0_fun/ppermute | solution.py:664
  11.3 10.7 %interior.3.inner_ref = f32[2,96,96]{2,1,0:T(8,128)S(1)} custom-call(s32[1]{0:T(128)} %bitcast.5.edge_ref, f32[2,16]{1,0:T(2,128)S(1)} %convert_element_type.0.table_ref, s32[2,4,8,128]{3,2,1,0:T(8,128)S(1)} %copy-done.30, bf16[2,96,3,4,8,128]{5,4,3,2,1,0:T(8,128)(2,1)} %get-tuple-element.32.basis_ref, s32[1]{0:T(128)} %bitcast.token_ref.flags_ref), custom_call_target="tpu_custom_call" | custom-call | flops 1 | bytes 1 | tf_op jit(solution)/shard_map/cond/branch_0_fun/interior/pallas_call | solution.py:190
  22.8 1.3 collective-permute-start.46
  24.1 5.6 %collective-permute-done.46.head_ref = bf16[128,128]{1,0:T(8,128)(2,1)S(1)} collective-permute-done((bf16[128,128]{1,0:T(8,128)(2,1)S(1)}, bf16[128,128]{1,0:T(8,128)(2,1)S(1)}, u32[]{:S(2)}, u32[]{:S(2)}) %collective-permute-start.46) | collective-permute-done | bytes 32800 | tf_op jit(solution)/shard_map/cond/branch_0_fun/ppermute | solution.py:672
  29.7 1.0 copy-done.4
  31.5 1.3 copy-done.5
  32.8 4.5 %face.6 = f32[2,96,96]{2,1,0:T(8,128)S(1)} custom-call(s32[1]{0:T(128)} %bitcast.6.flags_ref, f32[2,16]{1,0:T(2,128)S(1)} %convert_element_type.0.table_ref, s32[2,4,8,128]{3,2,1,0:T(8,128)S(1)} %copy-done.30, bf16[2,288,8,128]{3,2,1,0:T(8,128)(2,1)S(1)} %get-tuple-element.44.last_ref, bf16[2,290,8,128]{3,2,1,0:T(8,128)(2,1)S(1)} %copy-done.5, ...), custom_call_target="tpu_custom_call" | custom-call | flops 1 | bytes 1 | tf_op jit(solution)/shard_map/cond/branch_0_fun/face/pallas_call | solution.py:268
  37.3 1.3 collective-permute-start.48
  39.3 5.5 %collective-permute-done.48 = f32[2,96,96]{2,1,0:T(8,128)S(1)} collective-permute-done((f32[2,96,96]{2,1,0:T(8,128)S(1)}, f32[2,96,96]{2,1,0:T(8,128)S(1)}, u32[]{:S(2)}, u32[]{:S(2)}) %collective-permute-start.48) | collective-permute-done | bytes 73760 | tf_op jit(solution)/shard_map/cond/branch_0_fun/ppermute | solution.py:687
  44.9 2.8 %collective-permute-start.49 = (f32[2,96,96]{2,1,0:T(8,128)S(1)}, f32[2,96,96]{2,1,0:T(8,128)S(1)}, u32[]{:S(2)}, u32[]{:S(2)}) collective-permute-start(f32[2,96,96]{2,1,0:T(8,128)S(1)} %add.65.rest_0_.refs_2_), channel_id=1, source_target_pairs={{2,0},{10,8},{18,16},{26,24}} | collective-permute-start | bytes 221192 | tf_op jit(solution)/shard_map/cond/branch_0_fun/ppermute | solution.py:687
  48.3 1.6 collective-permute-done.49.rest_1_.refs_3_
  50.5 1.7 %assemble.3 = f32[128,128]{1,0:T(8,128)} custom-call(s32[2]{0:T(128)} %pad_add_fusion.2.flags_ref, s32[1]{0:T(128)} %bitcast.token_ref.flags_ref, s32[2,96,1]{2,1,0:T(8,128)} %copy.16.column_ids_ref, s32[2,1,96]{2,1,0:T(1,128)S(1)} %bitcast.35, bf16[12288,128]{1,0:T(8,128)(2,1)} %get-tuple-element.33.slab_ref, bf16[128,128]{1,0:T(8,128)(2,1)} %copy-done.60, ...), custom_call_target="tpu_custom_call" | custom-call | flops 1 | bytes 1 | tf_op jit(solution)/shard_map/cond/branch_0_fun/assemble/pallas_call | solution.py:325
  52.2 1.8 %collective-permute-start.59 = (bf16[6144,128]{1,0:T(8,128)(2,1)}, bf16[6144,128]{1,0:T(8,128)(2,1)}, u32[]{:S(2)}, u32[]{:S(2)}) collective-permute-start(bf16[6144,128]{1,0:T(8,128)(2,1)} %copy-done.22), channel_id=1, source_target_pairs={{0,1},{4,5},{8,9},{12,13},{16,17},{20,21},{24,25},{28,29}} | collective-permute-start | bytes 4718600 | tf_op jit(solution)/shard_map/cond/branch_0_fun/ppermute | solution.py:649
  54.0 1.7 %collective-permute-start.52 = (bf16[2,290,8,128]{3,2,1,0:T(8,128)(2,1)}, bf16[2,290,8,128]{3,2,1,0:T(8,128)(2,1)}, u32[]{:S(2)}, u32[]{:S(2)}) collective-permute-start(bf16[2,290,8,128]{3,2,1,0:T(8,128)(2,1)} %get-tuple-element.60), channel_id=1, source_target_pairs={{5,4},{6,5},{7,6},{13,12},{14,13},{15,14},{21,20},{22,21},{23,22},... | collective-permute-start | bytes 3563528 | tf_op jit(solution)/shard_map/cond/branch_0_fun/ppermute | solution.py:664
  55.7 2.4 %collective-permute-start.50 = (f32[128,128]{1,0:T(8,128)}, f32[128,128]{1,0:T(8,128)S(1)}, u32[]{:S(2)}, u32[]{:S(2)}) collective-permute-start(f32[128,128]{1,0:T(8,128)} %assemble.3), channel_id=1, source_target_pairs={{0,16},{9,25},{18,2},{27,11}} | collective-permute-start | bytes 196616 | tf_op jit(solution)/shard_map/cond/branch_0_fun/ppermute | solution.py:743
  58.1 2.2 %collective-permute-done.50 = f32[128,128]{1,0:T(8,128)S(1)} collective-permute-done((f32[128,128]{1,0:T(8,128)}, f32[128,128]{1,0:T(8,128)S(1)}, u32[]{:S(2)}, u32[]{:S(2)}) %collective-permute-start.50) | collective-permute-done | bytes 65568 | tf_op jit(solution)/shard_map/cond/branch_0_fun/ppermute | solution.py:743
  60.3 0.9 add.66
  61.1 4.9 %collective-permute-start.51 = (f32[128,128]{1,0:T(8,128)S(1)}, f32[128,128]{1,0:T(8,128)S(1)}, u32[]{:S(2)}, u32[]{:S(2)}) collective-permute-start(f32[128,128]{1,0:T(8,128)S(1)} %add.66), channel_id=1, source_target_pairs={{0,8},{16,24},{9,1},{25,17},{18,26},{2,10},{27,19},{11,3}} | collective-permute-start | bytes 196616 | tf_op jit(solution)/shard_map/cond/branch_0_fun/ppermute | solution.py:743
  68.0 1.3 collective-permute-start.53
  69.3 0.9 collective-permute-done.53.refs_1_
  70.2 1.3 collective-permute-start.64
  73.4 1.8 %factorize.3 = (bf16[384,128]{1,0:T(8,128)(2,1)}, f32[128,128]{1,0:T(8,128)}, f32[2,96,96]{2,1,0:T(8,128)}) custom-call(s32[2]{0:T(128)} %pad_add_fusion.1.flags_ref, s32[1]{0:T(128)} %bitcast.token_ref.flags_ref, f32[128,128]{1,0:T(8,128)} %copy-done.47, f32[128,128]{1,0:T(8,128)} %copy-done.56, f32[2,96,96]{2,1,0:T(8,128)} %copy-done.34, ...), custom_call_target="tpu_custom_call" | custom-call | flops 1 | bytes 1 | tf_op jit(solution)/shard_map/cond/branch_0_fun/factorize/pallas_call | solution.py:397
  75.3 1.5 fusion
  76.8 1.3 collective-permute-start.63
  78.8 1.3 collective-permute-start.57
  81.4 27.2 %collective-permute-done.57.rest_2_ = bf16[384,128]{1,0:T(8,128)(2,1)S(1)} collective-permute-done((bf16[384,128]{1,0:T(8,128)(2,1)S(1)}, bf16[384,128]{1,0:T(8,128)(2,1)S(1)}, u32[]{:S(2)}, u32[]{:S(2)}) %collective-permute-start.57) | collective-permute-done | bytes 98336 | tf_op jit(solution)/shard_map/cond/branch_0_fun/ppermute | solution.py:754
  109.9 2.9 %collective-permute-start.68 = (bf16[6144,128]{1,0:T(8,128)(2,1)}, bf16[6144,128]{1,0:T(8,128)(2,1)}, u32[]{:S(2)}, u32[]{:S(2)}) collective-permute-start(bf16[6144,128]{1,0:T(8,128)(2,1)} %collective-permute-done.64.rest_1_), channel_id=1, source_target_pairs={{2,1},{6,5},{10,9},{14,13},{18,17},{22,21},{26,25},{30,29}} | collective-permute-start | bytes 4718600 | tf_op jit(solution)/shard_map/cond/branch_0_fun/ppermute | solution.py:649
  112.7 5.2 %collective-permute-done.63.rest_1_ = bf16[3072,128]{1,0:T(8,128)(2,1)} collective-permute-done((bf16[3072,128]{1,0:T(8,128)(2,1)S(1)}, bf16[3072,128]{1,0:T(8,128)(2,1)}, u32[]{:S(2)}, u32[]{:S(2)}) %collective-permute-start.63) | collective-permute-done | bytes 786464 | tf_op jit(solution)/shard_map/cond/branch_0_fun/ppermute | solution.py:649
  117.9 2.2 %collective-permute-start.66 = (bf16[3072,128]{1,0:T(8,128)(2,1)}, bf16[3072,128]{1,0:T(8,128)(2,1)}, u32[]{:S(2)}, u32[]{:S(2)}) collective-permute-start(bf16[3072,128]{1,0:T(8,128)(2,1)} %collective-permute-done.63.rest_1_), channel_id=1, source_target_pairs={{2,3},{6,7},{10,11},{14,15},{18,19},{22,23},{26,27},{30,31}} | collective-permute-start | bytes 2359304 | tf_op jit(solution)/shard_map/cond/branch_0_fun/ppermute | solution.py:649
  120.1 1.3 collective-permute-start.65
  121.6 0.8 copy-done.6
  122.4 0.9 copy-done.14
  123.3 0.9 copy-done.17
  124.2 0.9 copy-done.19
  125.1 0.9 copy-done.21
  126.0 1.0 prepare.3
  127.0 4.7 %collective-permute-done.66.rest_2_ = bf16[3072,128]{1,0:T(8,128)(2,1)} collective-permute-done((bf16[3072,128]{1,0:T(8,128)(2,1)}, bf16[3072,128]{1,0:T(8,128)(2,1)}, u32[]{:S(2)}, u32[]{:S(2)}) %collective-permute-start.66) | collective-permute-done | bytes 786464 | tf_op jit(solution)/shard_map/cond/branch_0_fun/ppermute | solution.py:649
  131.7 4.9 %panel.8 = (bf16[12288,128]{1,0:T(8,128)(2,1)}, s32[1]{0:T(128)}) custom-call(s32[4]{0:T(128)S(1)} %pad_add_fusion.flags_ref, s32[1]{0:T(128)} %bitcast.token_ref.flags_ref, bf16[128,128]{1,0:T(8,128)(2,1)S(1)} %get-tuple-element.96.lower_ref, bf16[512,256]{1,0:T(8,128)(2,1)S(1)} %get-tuple-element.97.weights_ref, ...), custom_call_target="tpu_custom_call" | custom-call | flops 1 | bytes 1 | tf_op jit(solution)/shard_map/cond/branch_0_fun/panel/pallas_call | solution.py:576
  136.5 4.4 %collective-permute-start.69 = (bf16[3072,128]{1,0:T(8,128)(2,1)}, bf16[3072,128]{1,0:T(8,128)(2,1)S(1)}, u32[]{:S(2)}, u32[]{:S(2)}) collective-permute-start(bf16[3072,128]{1,0:T(8,128)(2,1)} %collective-permute-done.65.rest_1_), channel_id=1, source_target_pairs={{2,3},{6,7},{10,11},{14,15},{18,19},{22,23},{26,27},{30,31}} | collective-permute-start | bytes 2359304 | tf_op jit(solution)/shard_map/cond/branch_0_fun/ppermute | solution.py:649
  141.0 2.2 %added.3 = f32[128,128]{1,0:T(8,128)} custom-call(s32[1]{0:T(128)} %bitcast.token_ref.flags_ref, s32[1]{0:T(128)} %get-tuple-element.102.token_ref, s32[2,96,1]{2,1,0:T(8,128)} %copy.16.column_ids_ref, s32[2,1,96]{2,1,0:T(1,128)S(1)} %bitcast.36, f32[2,96,96]{2,1,0:T(8,128)} %get-tuple-element.84.sum_ref), custom_call_target="tpu_custom_call" | custom-call | flops 1 | bytes 1 | tf_op jit(solution)/shard_map/cond/branch_0_fun/added/pallas_call | solution.py:468
  143.2 1.3 collective-permute-start.67
  145.2 1.3 collective-permute-start.61
  146.5 4.0 %collective-permute-done.67.added_ref = f32[128,128]{1,0:T(8,128)S(1)} collective-permute-done((f32[128,128]{1,0:T(8,128)}, f32[128,128]{1,0:T(8,128)S(1)}, u32[]{:S(2)}, u32[]{:S(2)}) %collective-permute-start.67) | collective-permute-done | bytes 65568 | tf_op jit(solution)/shard_map/cond/branch_0_fun/ppermute | solution.py:713
  151.9 8.5 %panel.9 = (bf16[12288,128]{1,0:T(8,128)(2,1)}, s32[1]{0:T(128)}) custom-call(s32[4]{0:T(128)S(1)} %pad_add_fusion.flags_ref, s32[1]{0:T(128)} %get-tuple-element.102.token_ref, bf16[128,128]{1,0:T(8,128)(2,1)S(1)} %copy-done.10, bf16[512,256]{1,0:T(8,128)(2,1)S(1)} %get-tuple-element.97.weights_ref, ...), custom_call_target="tpu_custom_call", output_to_operand_aliasing={{0}: (10, {})} | custom-call | flops 1 | bytes 1 | tf_op jit(solution)/shard_map/cond/branch_0_fun/panel/pallas_call | solution.py:576
  161.2 5.1 %panel.10 = (bf16[12288,128]{1,0:T(8,128)(2,1)}, s32[1]{0:T(128)}) custom-call(s32[4]{0:T(128)S(1)} %pad_add_fusion.flags_ref, s32[1]{0:T(128)} %get-tuple-element.109.token_ref, bf16[128,128]{1,0:T(8,128)(2,1)S(1)} %copy-done.10, bf16[512,256]{1,0:T(8,128)(2,1)S(1)} %get-tuple-element.97.weights_ref, ...), custom_call_target="tpu_custom_call", output_to_operand_aliasing={{0}: (10, {})} | custom-call | flops 1 | bytes 1 | tf_op jit(solution)/shard_map/cond/branch_0_fun/panel/pallas_call | solution.py:576
  (79 shorter events, 14.2 us)
Async XLA Ops:
  2.0 9.3 %copy-start.30 = (s32[2,4,8,128]{3,2,1,0:T(8,128)S(1)}, s32[2,4,8,128]{3,2,1,0:T(8,128)}, u32[]{:S(2)}) copy-start(s32[2,4,8,128]{3,2,1,0:T(8,128)} %get-tuple-element.31.ids_ref) | copy-start | bytes 98308 | tf_op jit(solution)/shard_map/cond
  7.8 1.2 copy-start.22
  8.9 20.7 %collective-permute-start.45 = (bf16[2,290,8,128]{3,2,1,0:T(8,128)(2,1)}, bf16[2,290,8,128]{3,2,1,0:T(8,128)(2,1)S(1)}, u32[]{:S(2)}, u32[]{:S(2)}) collective-permute-start(bf16[2,290,8,128]{3,2,1,0:T(8,128)(2,1)} %get-tuple-element.60), channel_id=1, source_target_pairs={{1,0},{2,1},{3,2},{9,8},{10,9},{11,10},{17,16},{18,17},{19,18},{25... | collective-permute-start | bytes 3563528 | tf_op jit(solution)/shard_map/cond/branch_0_fun/ppermute | solution.py:664
  22.0 16.5 %copy-start.52 = (s32[2,96]{1,0:T(2,128)S(1)}, s32[2,96]{1,0:T(2,128)}, u32[]{:S(2)}) copy-start(s32[2,96]{1,0:T(2,128)} %get-tuple-element.52) | copy-start | bytes 2308 | tf_op jit(solution)/shard_map/cond
  22.8 6.8 %collective-permute-start.46 = (bf16[128,128]{1,0:T(8,128)(2,1)S(1)}, bf16[128,128]{1,0:T(8,128)(2,1)S(1)}, u32[]{:S(2)}, u32[]{:S(2)}) collective-permute-start(bf16[128,128]{1,0:T(8,128)(2,1)S(1)} %slice.16), channel_id=1, source_target_pairs={{8,9},{16,18},{24,27}} | collective-permute-start | bytes 98312 | tf_op jit(solution)/shard_map/cond/branch_0_fun/ppermute | solution.py:672
  29.7 20.2 %copy-start.60 = (bf16[128,128]{1,0:T(8,128)(2,1)}, bf16[128,128]{1,0:T(8,128)(2,1)S(1)}, u32[]{:S(2)}) copy-start(bf16[128,128]{1,0:T(8,128)(2,1)S(1)} %collective-permute-done.46.head_ref) | copy-start | bytes 98308 | tf_op jit(solution)/shard_map/cond
  29.7 1.1 copy-start.4
  30.7 39.5 %collective-permute-start.47 = (bf16[6144,128]{1,0:T(8,128)(2,1)}, bf16[6144,128]{1,0:T(8,128)(2,1)S(1)}, u32[]{:S(2)}, u32[]{:S(2)}) collective-permute-start(bf16[6144,128]{1,0:T(8,128)(2,1)} %get-tuple-element.43), channel_id=1, source_target_pairs={{0,3},{4,7},{8,11},{12,15},{16,19},{20,23},{24,27},{28,31}} | collective-permute-start | bytes 4718600 | tf_op jit(solution)/shard_map/cond/branch_0_fun/ppermute | solution.py:649
  31.5 1.3 copy-start.5
  37.3 7.6 %collective-permute-start.48 = (f32[2,96,96]{2,1,0:T(8,128)S(1)}, f32[2,96,96]{2,1,0:T(8,128)S(1)}, u32[]{:S(2)}, u32[]{:S(2)}) collective-permute-start(f32[2,96,96]{2,1,0:T(8,128)S(1)} %face.6), channel_id=1, source_target_pairs={{1,0},{3,2},{9,8},{11,10},{17,16},{19,18},{25,24},{27,26}} | collective-permute-start | bytes 221192 | tf_op jit(solution)/shard_map/cond/branch_0_fun/ppermute | solution.py:687
  44.9 5.0 %copy-start.34 = (f32[2,96,96]{2,1,0:T(8,128)}, f32[2,96,96]{2,1,0:T(8,128)S(1)}, u32[]{:S(2)}) copy-start(f32[2,96,96]{2,1,0:T(8,128)S(1)} %add.65.rest_0_.refs_2_) | copy-start | bytes 221188 | tf_op jit(solution)/shard_map/cond
  44.9 5.0 %collective-permute-start.49 = (f32[2,96,96]{2,1,0:T(8,128)S(1)}, f32[2,96,96]{2,1,0:T(8,128)S(1)}, u32[]{:S(2)}, u32[]{:S(2)}) collective-permute-start(f32[2,96,96]{2,1,0:T(8,128)S(1)} %add.65.rest_0_.refs_2_), channel_id=1, source_target_pairs={{2,0},{10,8},{18,16},{26,24}} | collective-permute-start | bytes 221192 | tf_op jit(solution)/shard_map/cond/branch_0_fun/ppermute | solution.py:687
  52.2 23.1 %collective-permute-start.59 = (bf16[6144,128]{1,0:T(8,128)(2,1)}, bf16[6144,128]{1,0:T(8,128)(2,1)}, u32[]{:S(2)}, u32[]{:S(2)}) collective-permute-start(bf16[6144,128]{1,0:T(8,128)(2,1)} %copy-done.22), channel_id=1, source_target_pairs={{0,1},{4,5},{8,9},{12,13},{16,17},{20,21},{24,25},{28,29}} | collective-permute-start | bytes 4718600 | tf_op jit(solution)/shard_map/cond/branch_0_fun/ppermute | solution.py:649
  54.0 12.1 %collective-permute-start.52 = (bf16[2,290,8,128]{3,2,1,0:T(8,128)(2,1)}, bf16[2,290,8,128]{3,2,1,0:T(8,128)(2,1)}, u32[]{:S(2)}, u32[]{:S(2)}) collective-permute-start(bf16[2,290,8,128]{3,2,1,0:T(8,128)(2,1)} %get-tuple-element.60), channel_id=1, source_target_pairs={{5,4},{6,5},{7,6},{13,12},{14,13},{15,14},{21,20},{22,21},{23,22},... | collective-permute-start | bytes 3563528 | tf_op jit(solution)/shard_map/cond/branch_0_fun/ppermute | solution.py:664
  55.7 4.6 %collective-permute-start.50 = (f32[128,128]{1,0:T(8,128)}, f32[128,128]{1,0:T(8,128)S(1)}, u32[]{:S(2)}, u32[]{:S(2)}) collective-permute-start(f32[128,128]{1,0:T(8,128)} %assemble.3), channel_id=1, source_target_pairs={{0,16},{9,25},{18,2},{27,11}} | collective-permute-start | bytes 196616 | tf_op jit(solution)/shard_map/cond/branch_0_fun/ppermute | solution.py:743
  61.1 6.8 %collective-permute-start.51 = (f32[128,128]{1,0:T(8,128)S(1)}, f32[128,128]{1,0:T(8,128)S(1)}, u32[]{:S(2)}, u32[]{:S(2)}) collective-permute-start(f32[128,128]{1,0:T(8,128)S(1)} %add.66), channel_id=1, source_target_pairs={{0,8},{16,24},{9,1},{25,17},{18,26},{2,10},{27,19},{11,3}} | collective-permute-start | bytes 196616 | tf_op jit(solution)/shard_map/cond/branch_0_fun/ppermute | solution.py:743
  66.7 2.6 %collective-permute-start.54 = (f32[2,96,96]{2,1,0:T(8,128)S(1)}, f32[2,96,96]{2,1,0:T(8,128)S(1)}, u32[]{:S(2)}, u32[]{:S(2)}) collective-permute-start(f32[2,96,96]{2,1,0:T(8,128)S(1)} %face.7), channel_id=1, source_target_pairs={{5,4},{7,6},{13,12},{15,14},{21,20},{23,22},{29,28},{31,30}} | collective-permute-start | bytes 221192 | tf_op jit(solution)/shard_map/cond/branch_0_fun/ppermute | solution.py:687
  68.0 4.8 %copy-start.47 = (f32[128,128]{1,0:T(8,128)}, f32[128,128]{1,0:T(8,128)S(1)}, u32[]{:S(2)}) copy-start(f32[128,128]{1,0:T(8,128)S(1)} %add.67.refs_0_) | copy-start | bytes 196612 | tf_op jit(solution)/shard_map/cond
  68.0 2.2 %collective-permute-start.53 = (f32[128,128]{1,0:T(8,128)S(1)}, f32[128,128]{1,0:T(8,128)S(1)}, u32[]{:S(2)}, u32[]{:S(2)}) collective-permute-start(f32[128,128]{1,0:T(8,128)S(1)} %add.67.refs_0_), channel_id=1, source_target_pairs={{0,4},{8,12},{16,20},{24,28},{9,13},{1,5},{25,29},{17,21},{18,22},... | collective-permute-start | bytes 196616 | tf_op jit(solution)/shard_map/cond/branch_0_fun/ppermute | solution.py:743
  70.2 2.6 %copy-start.56 = (f32[128,128]{1,0:T(8,128)}, f32[128,128]{1,0:T(8,128)S(1)}, u32[]{:S(2)}) copy-start(f32[128,128]{1,0:T(8,128)S(1)} %collective-permute-done.53.refs_1_) | copy-start | bytes 196612 | tf_op jit(solution)/shard_map/cond
  70.2 39.7 %collective-permute-start.64 = (bf16[6144,128]{1,0:T(8,128)(2,1)S(1)}, bf16[6144,128]{1,0:T(8,128)(2,1)}, u32[]{:S(2)}, u32[]{:S(2)}) collective-permute-start(bf16[6144,128]{1,0:T(8,128)(2,1)S(1)} %collective-permute-done.47.rest_2_), channel_id=1, source_target_pairs={{3,2},{7,6},{11,10},{15,14},{19,18},{23,22},{27,26},{31,30}} | collective-permute-start | bytes 4718600 | tf_op jit(solution)/shard_map/cond/branch_0_fun/ppermute | solution.py:649
  71.5 1.3 copy-start.40
  71.5 1.3 collective-permute-start.55
  75.3 2.8 %copy-start.13 = (bf16[384,128]{1,0:T(8,128)(2,1)S(1)}, bf16[384,128]{1,0:T(8,128)(2,1)}, u32[]{:S(2)}) copy-start(bf16[384,128]{1,0:T(8,128)(2,1)} %get-tuple-element.75.rest_0_) | copy-start | bytes 294916 | tf_op jit(solution)/shard_map/cond
  76.8 41.1 %collective-permute-start.63 = (bf16[3072,128]{1,0:T(8,128)(2,1)S(1)}, bf16[3072,128]{1,0:T(8,128)(2,1)}, u32[]{:S(2)}, u32[]{:S(2)}) collective-permute-start(bf16[3072,128]{1,0:T(8,128)(2,1)S(1)} %get-tuple-element.85.rest_0_), channel_id=1, source_target_pairs={{1,2},{5,6},{9,10},{13,14},{17,18},{21,22},{25,26},{29,30}} | collective-permute-start | bytes 2359304 | tf_op jit(solution)/shard_map/cond/branch_0_fun/ppermute | solution.py:649
  78.1 2.7 %collective-permute-start.58 = (bf16[384,128]{1,0:T(8,128)(2,1)S(1)}, bf16[384,128]{1,0:T(8,128)(2,1)S(1)}, u32[]{:S(2)}, u32[]{:S(2)}) collective-permute-start(bf16[384,128]{1,0:T(8,128)(2,1)S(1)} %copy-done.13), channel_id=1, source_target_pairs={{0,1},{4,5},{8,9},{12,13},{16,17},{20,21},{24,25},{28,29}} | collective-permute-start | bytes 294920 | tf_op jit(solution)/shard_map/cond/branch_0_fun/ppermute | solution.py:754
  78.8 29.8 %collective-permute-start.57 = (bf16[384,128]{1,0:T(8,128)(2,1)S(1)}, bf16[384,128]{1,0:T(8,128)(2,1)S(1)}, u32[]{:S(2)}, u32[]{:S(2)}) collective-permute-start(bf16[384,128]{1,0:T(8,128)(2,1)S(1)} %copy-done.13), channel_id=1, source_target_pairs={{0,2},{4,6},{8,10},{12,14},{16,18},{20,22},{24,26},{28,30}} | collective-permute-start | bytes 294920 | tf_op jit(solution)/shard_map/cond/branch_0_fun/ppermute | solution.py:754
  80.1 29.2 %collective-permute-start.56 = (bf16[384,128]{1,0:T(8,128)(2,1)S(1)}, bf16[384,128]{1,0:T(8,128)(2,1)S(1)}, u32[]{:S(2)}, u32[]{:S(2)}) collective-permute-start(bf16[384,128]{1,0:T(8,128)(2,1)S(1)} %copy-done.13), channel_id=1, source_target_pairs={{0,3},{4,7},{8,11},{12,15},{16,19},{20,23},{24,27},{28,31}} | collective-permute-start | bytes 294920 | tf_op jit(solution)/shard_map/cond/branch_0_fun/ppermute | solution.py:754
  80.7 0.6 copy-start.16
  109.2 0.7 copy-start.20
  109.9 41.3 %collective-permute-start.68 = (bf16[6144,128]{1,0:T(8,128)(2,1)}, bf16[6144,128]{1,0:T(8,128)(2,1)}, u32[]{:S(2)}, u32[]{:S(2)}) collective-permute-start(bf16[6144,128]{1,0:T(8,128)(2,1)} %collective-permute-done.64.rest_1_), channel_id=1, source_target_pairs={{2,1},{6,5},{10,9},{14,13},{18,17},{22,21},{26,25},{30,29}} | collective-permute-start | bytes 4718600 | tf_op jit(solution)/shard_map/cond/branch_0_fun/ppermute | solution.py:649
  117.9 13.7 %collective-permute-start.66 = (bf16[3072,128]{1,0:T(8,128)(2,1)}, bf16[3072,128]{1,0:T(8,128)(2,1)}, u32[]{:S(2)}, u32[]{:S(2)}) collective-permute-start(bf16[3072,128]{1,0:T(8,128)(2,1)} %collective-permute-done.63.rest_1_), channel_id=1, source_target_pairs={{2,3},{6,7},{10,11},{14,15},{18,19},{22,23},{26,27},{30,31}} | collective-permute-start | bytes 2359304 | tf_op jit(solution)/shard_map/cond/branch_0_fun/ppermute | solution.py:649
  120.1 16.5 %collective-permute-start.65 = (bf16[3072,128]{1,0:T(8,128)(2,1)S(1)}, bf16[3072,128]{1,0:T(8,128)(2,1)}, u32[]{:S(2)}, u32[]{:S(2)}) collective-permute-start(bf16[3072,128]{1,0:T(8,128)(2,1)S(1)} %get-tuple-element.90.rest_0_), channel_id=1, source_target_pairs={{1,2},{5,6},{9,10},{13,14},{17,18},{21,22},{25,26},{29,30}} | collective-permute-start | bytes 2359304 | tf_op jit(solution)/shard_map/cond/branch_0_fun/ppermute | solution.py:649
  121.6 0.8 copy-start.6
  122.4 0.9 copy-start.14
  123.3 0.9 copy-start.17
  124.2 0.9 copy-start.19
  125.1 0.9 copy-start.21
  127.0 9.5 %copy-start.9 = (bf16[128,128]{1,0:T(8,128)(2,1)}, bf16[128,128]{1,0:T(8,128)(2,1)S(1)}, u32[]{:S(2)}) copy-start(bf16[128,128]{1,0:T(8,128)(2,1)S(1)} %get-tuple-element.96.lower_ref) | copy-start | bytes 98308 | tf_op jit(solution)/shard_map/cond
  136.5 24.6 %collective-permute-start.69 = (bf16[3072,128]{1,0:T(8,128)(2,1)}, bf16[3072,128]{1,0:T(8,128)(2,1)S(1)}, u32[]{:S(2)}, u32[]{:S(2)}) collective-permute-start(bf16[3072,128]{1,0:T(8,128)(2,1)} %collective-permute-done.65.rest_1_), channel_id=1, source_target_pairs={{2,3},{6,7},{10,11},{14,15},{18,19},{22,23},{26,27},{30,31}} | collective-permute-start | bytes 2359304 | tf_op jit(solution)/shard_map/cond/branch_0_fun/ppermute | solution.py:649
  143.2 7.3 %collective-permute-start.67 = (f32[128,128]{1,0:T(8,128)}, f32[128,128]{1,0:T(8,128)S(1)}, u32[]{:S(2)}, u32[]{:S(2)}) collective-permute-start(f32[128,128]{1,0:T(8,128)} %added.3), channel_id=1, source_target_pairs={{8,9},{16,18},{24,27}} | collective-permute-start | bytes 196616 | tf_op jit(solution)/shard_map/cond/branch_0_fun/ppermute | solution.py:713
  144.5 16.0 %collective-permute-start.62 = (f32[2,96,96]{2,1,0:T(8,128)}, f32[2,96,96]{2,1,0:T(8,128)S(1)}, u32[]{:S(2)}, u32[]{:S(2)}) collective-permute-start(f32[2,96,96]{2,1,0:T(8,128)} %get-tuple-element.84.sum_ref), channel_id=1, source_target_pairs={{0,1},{4,5},{8,9},{12,13},{16,17},{20,21},{24,25},{28,29}} | collective-permute-start | bytes 221192 | tf_op jit(solution)/shard_map/cond/branch_0_fun/ppermute | solution.py:759
  145.2 15.3 %collective-permute-start.61 = (f32[2,96,96]{2,1,0:T(8,128)}, f32[2,96,96]{2,1,0:T(8,128)S(1)}, u32[]{:S(2)}, u32[]{:S(2)}) collective-permute-start(f32[2,96,96]{2,1,0:T(8,128)} %get-tuple-element.84.sum_ref), channel_id=1, source_target_pairs={{0,2},{4,6},{8,10},{12,14},{16,18},{20,22},{24,26},{28,30}} | collective-permute-start | bytes 221192 | tf_op jit(solution)/shard_map/cond/branch_0_fun/ppermute | solution.py:759
  150.5 10.0 %collective-permute-start.60 = (f32[2,96,96]{2,1,0:T(8,128)}, f32[2,96,96]{2,1,0:T(8,128)S(1)}, u32[]{:S(2)}, u32[]{:S(2)}) collective-permute-start(f32[2,96,96]{2,1,0:T(8,128)} %get-tuple-element.84.sum_ref), channel_id=1, source_target_pairs={{0,3},{4,7},{8,11},{12,15},{16,19},{20,23},{24,27},{28,31}} | collective-permute-start | bytes 221192 | tf_op jit(solution)/shard_map/cond/branch_0_fun/ppermute | solution.py:759
  151.1 0.8 copy-start.10
  151.9 8.6 %copy-start.42 = (f32[2,96,96]{2,1,0:T(8,128)S(1)}, f32[2,96,96]{2,1,0:T(8,128)}, u32[]{:S(2)}) copy-start(f32[2,96,96]{2,1,0:T(8,128)} %get-tuple-element.84.sum_ref) | copy-start | bytes 221188 | tf_op jit(solution)/shard_map/cond
  151.9 9.3 %copy-start.7 = (f32[128,128]{1,0:T(8,128)S(1)}, f32[128,128]{1,0:T(8,128)}, u32[]{:S(2)}) copy-start(f32[128,128]{1,0:T(8,128)} %get-tuple-element.92.head_ref.added_ref) | copy-start | bytes 196612 | tf_op jit(solution)/shard_map/cond
  151.9 9.3 %copy-start.25 = (bf16[12288,128]{1,0:T(8,128)(2,1)S(1)}, bf16[12288,128]{1,0:T(8,128)(2,1)}, u32[]{:S(2)}) copy-start(bf16[12288,128]{1,0:T(8,128)(2,1)} %get-tuple-element.33.slab_ref) | copy-start | bytes 9437188 | tf_op jit(solution)/shard_map/cond
  (3 other events, 1.9 us)
